TPU v7x, 128 devices: a whole 4x4x4 slice. The times are simulated.
128 devices in a mesh: lat: 4 (over z_hi, core), lon: 32 (over z_lo, y, x).
Axes of the slice: x: 4, y: 4, z: 4 (z_hi: 2, z_lo: 2; z = z_hi * 2 + z_lo), core: 2. Of those that a mesh axis runs over, the one named last changes fastest.
Arguments:
- point_values: float32 [2, 8192, 256], P(None, ('lat', 'lon')), may hold values from -6 to 6
- theta_weights: bfloat16 [8192, 32, 256], P(('lat', 'lon')), may hold values from -1.796875 to 1.796875
- phi_weights: bfloat16 [8192, 128, 256], P(('lat', 'lon')), may hold values from -1.796875 to 1.796875
- block_counts: int32 [8192], P(('lat', 'lon')), may hold values from 0 to 256, as said below
- theta_offsets: int32 [8192], P(('lat', 'lon')), may hold values from 0 to 1024
- phi_offsets: int32 [8192], P(('lat', 'lon')), may hold values from 0 to 256
- conversion: bfloat16 [128, 4096, 2048], P(('lat', 'lon')), may hold values from -0.09375 to 0.09375
Outputs:
- coefficients: float32 [128, 2, 2048], P(('lat', 'lon'))
Inputs may be any that keep to these rules, and one draw needn't show every extreme that they name: `block_counts`: within the blocks of one tile, the blocks that hold points come first; the first block of every tile holds 256 points.
All inputs are finite; a program needn't handle non-finite values.
Results may differ from a plain program's by a relative error of at most 0.004.
Values sent between devices are 32-bit elements; how exact they have to be, the bound alone decides.
A program may use at most 192 MiB of HBM per device.

v0:
```python
import math

import jax
import jax.numpy as jnp
from jax import lax
from jax.sharding import PartitionSpec as P

GRID_ROWS = 4096
GRID_COLS = 8192
ORD_DEV = 1


def shifted(value, axis, by):
    size = lax.axis_size(axis)
    return lax.ppermute(value, axis, [(i, (i + by) % size) for i in range(size)])


def turn_table(indices, frequencies, period):
    phase = jnp.mod(indices[:, None] * frequencies[None, :], period).astype(jnp.float32) * (
        2.0 * math.pi / period
    )
    return (jnp.cos(phase), jnp.sin(phase))


def column_orders(columns, lat_count, lon_count):
    lon_place = columns // (lat_count * ORD_DEV)
    lat_place = columns // ORD_DEV % lat_count
    within = columns % ORD_DEV
    order_index = (lat_place * lon_count + lon_place) * ORD_DEV + within
    return order_index - ORD_DEV * lat_count * lon_count // 2


def phi_transform(cells, col_index, columns, lat_count, lon_count):
    highest = lax.Precision.HIGHEST
    cosines, sines = turn_table(col_index, column_orders(columns, lat_count, lon_count), GRID_COLS)
    real_part = jnp.einsum("tp,pc->ct", cells[0], cosines, precision=highest) + jnp.einsum(
        "tp,pc->ct", cells[1], sines, precision=highest
    )
    imag_part = jnp.einsum("tp,pc->ct", cells[1], cosines, precision=highest) - jnp.einsum(
        "tp,pc->ct", cells[0], sines, precision=highest
    )
    return jnp.stack([real_part, imag_part], axis=1)


def theta_transform(sums, row_index):
    highest = lax.Precision.HIGHEST
    frequencies = jnp.arange(GRID_ROWS, dtype=jnp.int32) - GRID_ROWS // 2
    cosines, sines = turn_table(row_index, frequencies, GRID_ROWS)
    real_part = jnp.einsum("ct,tk->ck", sums[:, 0], cosines, precision=highest) + jnp.einsum(
        "ct,tk->ck", sums[:, 1], sines, precision=highest
    )
    imag_part = jnp.einsum("ct,tk->ck", sums[:, 1], cosines, precision=highest) - jnp.einsum(
        "ct,tk->ck", sums[:, 0], sines, precision=highest
    )
    return jnp.stack([real_part, imag_part], axis=1)


def fold_margins(extended, rows_dev, cols_dev, win_rows, win_cols):
    moved_cols = shifted(extended[:, :, cols_dev:], "lon", 1)
    tile = extended[:, :, :cols_dev].at[:, :, :win_cols].add(moved_cols)
    moved_rows = shifted(tile[:, rows_dev:, :], "lat", 1)
    return tile[:, :rows_dev].at[:, :win_rows].add(moved_rows)


def shards(
    point_values, theta_weights, phi_weights, block_counts, theta_offsets, phi_offsets, conversion
):
    lat_count = lax.axis_size("lat")
    lon_count = lax.axis_size("lon")
    blocks_here, win_rows, points = theta_weights.shape
    win_cols = phi_weights.shape[1]
    rows_dev = GRID_ROWS // lat_count
    cols_dev = GRID_COLS // lon_count
    order_total = ORD_DEV * lat_count * lon_count
    unitary = 1.0 / math.sqrt(GRID_ROWS * GRID_COLS)
    highest = lax.Precision.HIGHEST
    alive = (jnp.arange(points, dtype=jnp.int32)[None, :] < block_counts[:, None]).astype(
        jnp.float32
    )
    weighted = (
        theta_weights[None].astype(jnp.float32) * (point_values * alive[None])[:, :, None, :]
    ).astype(jnp.bfloat16)
    windows = jnp.einsum(
        "xbrp,bqp->bxrq", weighted, phi_weights, preferred_element_type=jnp.float32
    )
    ext_rows = rows_dev + win_rows
    ext_cols = cols_dev + win_cols
    col_place = (
        jnp.arange(ext_cols, dtype=jnp.int32)[None, :, None] - phi_offsets[:, None, None]
        == jnp.arange(win_cols, dtype=jnp.int32)[None, None, :]
    ).astype(jnp.float32)
    placed = jnp.einsum("bxrq,bcq->bxrc", windows, col_place, precision=highest)
    row_place = (
        jnp.arange(ext_rows, dtype=jnp.int32)[:, None, None] - theta_offsets[None, :, None]
        == jnp.arange(win_rows, dtype=jnp.int32)[None, None, :]
    ).astype(jnp.float32)
    extended = jnp.einsum("tbr,bxrc->xtc", row_place, placed, precision=highest)
    tile = fold_margins(extended, rows_dev, cols_dev, win_rows, win_cols)
    banded = lax.all_to_all(tile, "lon", split_axis=1, concat_axis=2, tiled=True)
    every_order = phi_transform(
        banded,
        jnp.arange(GRID_COLS, dtype=jnp.int32),
        jnp.arange(order_total, dtype=jnp.int32),
        lat_count,
        lon_count,
    )
    by_rows = lax.all_to_all(every_order, "lon", split_axis=0, concat_axis=2, tiled=True)
    row_total = by_rows.shape[2]
    row_index = (
        lax.axis_index("lat") * rows_dev + jnp.arange(row_total, dtype=jnp.int32)
    ) % GRID_ROWS
    summed = lax.psum_scatter(
        theta_transform(by_rows, row_index), "lat", scatter_dimension=0, tiled=True
    )
    spectrum = (summed * unitary).astype(jnp.bfloat16)
    return jnp.einsum("oxk,okl->oxl", spectrum, conversion, preferred_element_type=jnp.float32)


def solution(mesh):
    placed = (
        P(None, ("lat", "lon"), None),
        P(("lat", "lon"), None, None),
        P(("lat", "lon"), None, None),
        P(("lat", "lon")),
        P(("lat", "lon")),
        P(("lat", "lon")),
        P(("lat", "lon"), None, None),
    )
    return jax.shard_map(
        shards, mesh=mesh, in_specs=placed, out_specs=P(("lat", "lon"), None, None), check_vma=False
    )
```

profile of v0, /device:TPU:1, one launch (start us, length us, event | category | flops | bytes accessed | tf_op | source)
XLA Modules:
  0.0 576.9 jit_solution(6876081924177748442)
XLA Ops:
  6.5 1.6 convert_element_type.32
  8.2 0.7 fusion.74
  8.9 0.9 broadcast_multiply_fusion
  9.8 0.1 copy.11
  9.9 0.7 iota_subtract_fusion.1
  10.7 0.7 iota_subtract_fusion
  11.4 1.2 fusion.8
  12.7 1.6 fusion.37
  14.2 15.7 %fusion.6 = f32[64,2,32,384]{3,2,1,0:T(8,128)S(1)} fusion(f32[64,2,32,128]{3,2,1,0:T(8,128)S(1)} %fusion.37, s32[64,384]{1,0:T(8,128)S(1)} %iota_subtract_fusion.1), kind=kOutput, calls=%fused_computation.12 | convolution fusion | flops 2419064832 | bytes 8486912 | tf_op jit(solution)/shard_map/bxrq,bcq->bxrc/dot_general | solution.py:92
  29.9 14.8 %fusion.42 = f32[2,1056,384]{2,1,0:T(8,128)S(1)} fusion(f32[64,2,32,384]{3,2,1,0:T(8,128)S(1)} %fusion.6, pred[1056,64,32,1]{0,1,2,3:T(32,128)(4,1)S(1)} %fusion.8), kind=kOutput, calls=%fused_computation.40 | convolution fusion | flops 19931332608 | bytes 11698176 | tf_op jit(solution)/shard_map/tbr,bxrc->xtc/dot_general | solution.py:97
  44.8 0.1 slice.92
  44.8 2.1 collective-permute-start
  46.9 0.2 slice.90
  47.1 28.5 %collective-permute-done = f32[2,1056,128]{2,1,0:T(8,128)S(1)} collective-permute-done((f32[2,1056,128]{2,1,0:T(8,128)S(1)}, f32[2,1056,128]{2,1,0:T(8,128)S(1)}, u32[]{:S(2)}, u32[]{:S(2)}) %collective-permute-start) | collective-permute-done | bytes 1081376 | tf_op jit(solution)/shard_map/ppermute | solution.py:15
  75.6 0.1 fusion.72
  75.7 4.5 collective-permute-start.1
  80.2 0.1 slice.93
  80.4 1.2 collective-permute-done.1
  81.6 3.0 copy.13
  84.5 4.2 all-to-all-start
  88.7 26.8 %all-to-all-done = f32[2,1024,256]{2,0,1:T(2,128)S(1)} async-done(((f32[2,1024,256]{2,0,1:T(2,128)}), f32[2,1024,256]{2,0,1:T(2,128)S(1)}, u32[]{:S(2)}, u32[]{:S(2)}) %all-to-all-start) | async-done | bytes 2097184 | tf_op jit(solution)/shard_map/all_to_all | solution.py:99
  115.5 1.2 copy.51
  116.7 0.2 fusion.128
  117.0 0.6 copy.25
  117.6 0.6 copy.26
  118.2 17.9 %fusion.54 = f32[128,32]{0,1:T(8,128)S(1)} fusion(f32[32,8192]{1,0:T(8,128)S(1)} %bitcast.75, s32[128]{0:T(128)S(1)} %fusion.93), kind=kOutput, calls=%fused_computation.48 | convolution fusion | flops 417333248 | bytes 1065472 | tf_op jit(solution)/shard_map/tp,pc->ct/dot_general | solution.py:36
  136.2 18.3 %fusion.52 = f32[128,32]{0,1:T(8,128)S(1)} fusion(f32[32,8192]{1,0:T(8,128)S(1)} %bitcast.77, s32[128]{0:T(128)S(1)} %fusion.93), kind=kOutput, calls=%fused_computation.47 | convolution fusion | flops 417333248 | bytes 1065472 | tf_op jit(solution)/shard_map/tp,pc->ct/dot_general | solution.py:39
  154.4 18.1 %fusion.63 = f32[128,1,32]{0,2,1:T(8,128)S(1)} fusion(f32[128,32]{0,1:T(8,128)S(1)} %fusion.54, f32[32,8192]{1,0:T(8,128)S(1)} %bitcast.78, s32[128]{0:T(128)S(1)} %fusion.93), kind=kOutput, calls=%fused_computation.52 | convolution fusion | flops 417337344 | bytes 1081856 | tf_op jit(solution)/shard_map/tp,pc->ct/dot_general | solution.py:36
  172.5 18.4 %fusion.69 = f32[128,1,32]{0,2,1:T(8,128)S(1)} fusion(f32[128,32]{0,1:T(8,128)S(1)} %fusion.52, f32[32,8192]{1,0:T(8,128)S(1)} %bitcast.76, s32[128]{0:T(128)S(1)} %fusion.93), kind=kOutput, calls=%fused_computation.54 | convolution fusion | flops 417337344 | bytes 1081856 | tf_op jit(solution)/shard_map/tp,pc->ct/dot_general | solution.py:39
  190.9 0.1 copy.15
  191.1 0.8 reshape.190
  191.8 5.7 all-to-all-start.1
  197.5 0.0 all-reduce.3.cloned.1.call-start
  197.6 7.1 %all-to-all-done.1 = f32[32,1,256]{2,1,0:T(1,128)S(1)} async-done(((f32[32,1,256]{2,1,0:T(1,128)}), f32[32,1,256]{2,1,0:T(1,128)S(1)}, u32[]{:S(2)}, u32[]{:S(2)}) %all-to-all-start.1) | async-done | bytes 32800 | tf_op jit(solution)/shard_map/all_to_all | solution.py:107
  204.7 0.5 broadcast.289
  205.2 0.7 reduce.4
  205.9 0.1 reshape.191
  206.1 0.1 all_to_all.30
  206.3 69.4 %fusion.15 = f32[4,4096]{1,0:T(4,128)S(1)} fusion(s32[4096]{0:T(1024)S(1)} %iota_add_fusion, s32[1024]{0:T(1024)S(1)} %add_select_fusion.2, f32[4,1,1024]{2,1,0:T(1,128)S(1)} %get-tuple-element.31), kind=kOutput, calls=%fused_computation.20 | convolution fusion | flops 260046848 | bytes 102400 | tf_op jit(solution)/shard_map/ct,tk->ck/dot_general | solution.py:49
  275.7 81.8 %fusion.13 = f32[4,4096]{1,0:T(4,128)S(1)} fusion(s32[4096]{0:T(1024)S(1)} %iota_add_fusion, s32[1024]{0:T(1024)S(1)} %add_select_fusion.2, f32[4,1,1024]{2,1,0:T(1,128)S(1)} %get-tuple-element.32), kind=kOutput, calls=%fused_computation.19 | convolution fusion | flops 260046848 | bytes 102400 | tf_op jit(solution)/shard_map/ct,tk->ck/dot_general | solution.py:52
  357.5 82.3 %fusion.25 = f32[4,1,4096]{2,0,1:T(4,128)S(1)} fusion(f32[4,4096]{1,0:T(4,128)S(1)} %fusion.15, s32[4096]{0:T(1024)S(1)} %iota_add_fusion, s32[1024]{0:T(1024)S(1)} %add_select_fusion.2, f32[4,1,1024]{2,1,0:T(1,128)S(1)} %get-tuple-element.32), kind=kOutput, calls=%fused_computation.28 | convolution fusion | flops 260063232 | bytes 167936 | tf_op jit(solution)/shard_map/ct,tk->ck/dot_general | solution.py:49
  439.8 0.0 copy-start.1
  439.9 82.5 %fusion.31 = f32[4,1,4096]{2,0,1:T(4,128)S(1)} fusion(f32[4,4096]{1,0:T(4,128)S(1)} %fusion.13, s32[4096]{0:T(1024)S(1)} %iota_add_fusion, s32[1024]{0:T(1024)S(1)} %add_select_fusion.2, f32[4,1,1024]{2,1,0:T(1,128)S(1)} %get-tuple-element.31), kind=kOutput, calls=%fused_computation.30 | convolution fusion | flops 260063232 | bytes 167936 | tf_op jit(solution)/shard_map/ct,tk->ck/dot_general | solution.py:52
  522.4 0.8 copy.18
  523.2 0.0 all-reduce.3.cloned.1.call-update
  523.2 0.6 dynamic-slice.16
  523.9 36.7 %all-reduce.3.cloned.1.call-done = f32[4,2,4096]{2,1,0:T(2,128)} async-done(((f32[4,2,4096]{2,1,0:T(2,128)}), f32[4,2,4096]{2,1,0:T(2,128)}) %all-reduce.3.cloned.1.call-update) | async-done | bytes 131088
  560.6 9.3 %fusion.45 = f32[1,2,2048]{2,1,0:T(2,128)} fusion(bf16[1,4096,2048]{2,1,0:T(8,128)(2,1)} %param.17, f32[4,2,4096]{2,1,0:T(2,128)} %all-reduce.3.cloned.1.call-done, u32[]{:T(128)} %bitcast.22), kind=kOutput, calls=%fused_computation.41 | convolution fusion | flops 33570816 | bytes 16826880 | tf_op jit(solution)/shard_map/oxk,okl->oxl/dot_general | solution.py:116
  (13 shorter events, 0.1 us)
Async XLA Ops:
  6.5 6.1 %copy-start = (bf16[64,128,256]{2,1,0:T(8,128)(2,1)S(1)}, bf16[64,128,256]{2,1,0:T(8,128)(2,1)}, u32[]{:S(2)}) copy-start(bf16[64,128,256]{2,1,0:T(8,128)(2,1)} %param.13) | copy-start | bytes 12582916
  44.8 30.8 %collective-permute-start = (f32[2,1056,128]{2,1,0:T(8,128)S(1)}, f32[2,1056,128]{2,1,0:T(8,128)S(1)}, u32[]{:S(2)}, u32[]{:S(2)}) collective-permute-start(f32[2,1056,128]{2,1,0:T(8,128)S(1)} %slice.92), channel_id=1, source_target_pairs={{0,1},{1,2},{2,3},{3,4},{4,5},{5,6},{6,7},{7,8},{8,9},{9,10},{10,1... | collective-permute-start | bytes 3244040 | tf_op jit(solution)/shard_map/ppermute | solution.py:15
  75.7 5.8 %collective-permute-start.1 = (f32[2,32,256]{2,1,0:T(8,128)S(1)}, f32[2,32,256]{2,1,0:T(8,128)S(1)}, u32[]{:S(2)}, u32[]{:S(2)}) collective-permute-start(f32[2,32,256]{2,1,0:T(8,128)S(1)} %slice.95), channel_id=1, source_target_pairs={{0,32},{32,64},{64,96},{96,0},{1,33},{33,65},{65,97},{97,1},{2,34}... | collective-permute-start | bytes 196616 | tf_op jit(solution)/shard_map/ppermute | solution.py:15
  84.5 31.0 %all-to-all-start = ((f32[2,1024,256]{2,0,1:T(2,128)}), f32[2,1024,256]{2,0,1:T(2,128)S(1)}, u32[]{:S(2)}, u32[]{:S(2)}) async-start(f32[2,1024,256]{2,0,1:T(2,128)} %copy.13), calls=%async_computation | async-start | bytes 4194304 | tf_op jit(solution)/shard_map/all_to_all | solution.py:99
  191.8 12.9 %all-to-all-start.1 = ((f32[32,1,256]{2,1,0:T(1,128)}), f32[32,1,256]{2,1,0:T(1,128)S(1)}, u32[]{:S(2)}, u32[]{:S(2)}) async-start(f32[32,1,256]{2,1,0:T(1,128)} %reshape.190), calls=%async_computation.1 | async-start | bytes 65536 | tf_op jit(solution)/shard_map/all_to_all | solution.py:107
  197.5 363.1 %all-reduce.3.cloned.1.call-start = ((), (), s32[]{:S(2)}) async-start(), calls=%async_computation.2 | async-start | bytes 262144
  439.8 83.4 %copy-start.1 = (u32[128]{0:T(128)S(1)}, u32[128]{0:T(128)}, u32[]{:S(2)}) copy-start(u32[128]{0:T(128)} %constant.167) | copy-start | bytes 1540
Sparse Core Ops, SparseCore 0:
  523.3 37.2 all-reduce.2
where the time goes:
time: 587 us; the launch traced here: 577 us
  matrix products  430 us (73%)
  waiting for transfers between devices  100 us (17%)
  starting transfers between devices  16.5 us (3%)
  between operations  13.9 us (2%)
  local copies, waits for them, and re-layouts  9.25 us (2%)
  other arithmetic  6.87 us (1%)
    dot_general x1, matrix products, theta_transform(): jnp.einsum('ct,tk->ck', sums[:, 0], sines, precision=highest)  82.5 us
    dot_general x1, matrix products, theta_transform(): jnp.einsum('ct,tk->ck', sums[:, 1], sines, precision=highest)  82.3 us
    dot_general x1, matrix products, theta_transform(): jnp.einsum('ct,tk->ck', sums[:, 1], cosines, precision=highest)  81.8 us
    dot_general x1, matrix products, theta_transform(): jnp.einsum('ct,tk->ck', sums[:, 0], cosines, precision=highest)  69.4 us
    unnamed x2, waiting for transfers between devices  36.7 us
    ppermute x2, waiting for transfers between devices, shifted(): lax.ppermute(value, axis, [(i, (i + by) % size) for i in range(size)])  29.7 us
    all_to_all x1, waiting for transfers between devices, shards(): lax.all_to_all(tile, 'lon', split_axis=1, concat_axis=2, tiled=True)  26.8 us
    dot_general x1, matrix products, phi_transform(): jnp.einsum('tp,pc->ct', cells[0], sines, precision=highest)  18.4 us
  transfers between devices with their start and end apart: 5, of which 5 were waited for; matrix products, arithmetic and copies ran while one was open for 0% of the time, Pallas kernels for 0%

commit v1 on v0

v1 whole, which is shorter than its diff:
```python
import functools
import math

import jax
import jax.numpy as jnp
import numpy as np
from jax import lax
from jax.experimental import pallas as pl
from jax.experimental.pallas import tpu as pltpu
from jax.sharding import PartitionSpec as P

GRID_ROWS = 4096
GRID_COLS = 8192
ORDERS = 128
BLOCKS = 64
WIN_ROWS = 32
WIN_COLS = 128
PTS = 256
ROWS_DEV = 1024
COLS_DEV = 256
EXT_ROWS = ROWS_DEV + WIN_ROWS
EXT_COLS = COLS_DEV + WIN_COLS
DEGREES = 2048
LANES = 128
T0 = 16
T1 = ROWS_DEV // T0
NX, NY, NZC = 4, 4, 8
CHUNK = 8
NCHUNK = BLOCKS // CHUNK
G_ROWS = T0 * LANES + LANES
MESH = pl.DeviceIdType.MESH
MIB = 1 << 20
BF16 = jnp.bfloat16
F32 = jnp.float32


def split_np(table):
    hi = table.astype(jnp.bfloat16)
    lo = (table - hi.astype(np.float64)).astype(jnp.bfloat16)
    return hi, lo


@functools.cache
def tables():
    place = np.arange(ORDERS)
    gx, gy, zc = place // 32, place // 8 % 4, place % 8
    order = zc * 16 + gy * 4 + gx - ORDERS // 2
    phase = (order[:, None] * np.arange(EXT_COLS)[None, :]) % GRID_COLS * (2 * np.pi / GRID_COLS)
    base = np.concatenate([np.cos(phase), np.sin(phase)]).astype(np.float32)
    turn = (order[:, None] * np.arange(32)[None, :]) % 32 * (2 * np.pi / 32)
    rot = np.zeros((ORDERS, LANES), np.float32)
    rot[:, :32] = np.cos(turn)
    rot[:, 32:64] = np.sin(turn)

    def rows_of(t1):
        angle = (t1[:, None] * np.arange(256)[None, :]) % 256 * (2 * np.pi / 256)
        return np.cos(angle), np.sin(angle)

    lane = np.arange(512)
    cos, sin = rows_of((lane // 128 * 64 + lane % 64) % 256)
    real = (lane % 128 < 64)[:, None]
    main = np.where(real, np.concatenate([cos, -sin], 1), np.concatenate([sin, cos], 1))
    cos, sin = rows_of(((lane // 128 + 1) * 64 + lane % 64 // 16) % 256)
    margin = np.where(real, np.concatenate([cos, -sin], 1), np.concatenate([sin, cos], 1))
    margin = margin * (lane % 64 < 32)[:, None]
    w_hi, w_lo = split_np(np.concatenate([main, margin]))

    unitary = 1.0 / math.sqrt(GRID_ROWS * GRID_COLS)
    angle = np.arange(16)[:, None] * np.arange(256)[None, :] * (2 * np.pi / 4096)
    twiddle = (np.concatenate([np.cos(angle), np.sin(angle)]) * unitary).astype(np.float32)

    angle = np.arange(16)[:, None] * np.arange(16)[None, :] % 16 * (2 * np.pi / 16)
    cos, sin = np.cos(angle), np.sin(angle)
    f_hi, f_lo = split_np(np.block([[cos, sin], [-sin, cos]]))
    last = np.concatenate([f_hi, f_lo, f_hi, np.zeros_like(f_hi)], 1)
    return base, rot, np.stack([w_hi, w_lo]), twiddle, last


def nt_dot(a, b):
    return lax.dot_general(a, b, (((1,), (1,)), ((), ())), preferred_element_type=F32)


def spread_kernel(counts, theta_offs, phi_offs, values, theta_hbm, phi_hbm, out, theta, phi, win, ext, sems):
    def fetch(c):
        part = pl.ds(c * CHUNK, CHUNK)
        return (
            pltpu.make_async_copy(theta_hbm.at[part], theta.at[part], sems.at[0, c]),
            pltpu.make_async_copy(phi_hbm.at[part], phi.at[part], sems.at[1, c]),
        )

    for c in range(NCHUNK):
        for copy in fetch(c):
            copy.start()

    def clear(i, carry):
        for k in range(4):
            for x in range(2):
                ext[k, x, pl.ds(pl.multiple_of(i * 96, 8), 96), :] = jnp.zeros((96, LANES), F32)
        return carry

    lax.fori_loop(0, EXT_ROWS // 96, clear, 0)
    point = lax.broadcasted_iota(jnp.int32, (1, PTS), 1)
    lane = lax.broadcasted_iota(jnp.int32, (WIN_ROWS, LANES), 1)

    def step(c, carry):
        for copy in fetch(c):
            copy.wait()
        for n in range(CHUNK):
            b = c * CHUNK + n
            live = point < counts[b]
            rows = theta[b].astype(F32)
            parts = []
            for x in range(2):
                own = jnp.where(live, values[x, pl.ds(b, 1), :], 0.0)
                parts.append((rows * own).astype(BF16))
            win[n] = nt_dot(jnp.concatenate(parts, 0), phi[b])
        for n in range(CHUNK):
            b = c * CHUNK + n
            row = theta_offs[b]
            col = phi_offs[b]
            tile = col // LANES
            shift = col % LANES
            near = lane >= shift
            for x in range(2):
                moved = pltpu.roll(win[n, x * WIN_ROWS : (x + 1) * WIN_ROWS, :], shift, 1)
                here = pl.ds(row, WIN_ROWS)
                ext[tile, x, here, :] += jnp.where(near, moved, 0.0)
                ext[tile + 1, x, here, :] += jnp.where(near, 0.0, moved)
        return carry

    lax.fori_loop(0, NCHUNK, step, 0)

    for k in range(3):
        cols = slice(k * LANES, (k + 1) * LANES)
        for x in range(2):
            for t0 in range(T0):
                at = t0 * LANES + x * T1
                out[at : at + T1, cols] = ext[k, x, pl.ds(t0, T1, stride=T0), :].astype(BF16)
            at = T0 * LANES + x * T1
            out[at : at + 32, cols] = ext[k, x, ROWS_DEV:EXT_ROWS, :].astype(BF16)
            out[at + 32 : at + 64, cols] = jnp.zeros((32, LANES), BF16)


def spread(point_values, theta_weights, phi_weights, block_counts, theta_offsets, phi_offsets):
    smem = pl.BlockSpec(memory_space=pltpu.SMEM)
    vmem = pl.BlockSpec(memory_space=pltpu.VMEM)
    hbm = pl.BlockSpec(memory_space=pl.ANY)
    return pl.pallas_call(
        spread_kernel,
        out_shape=jax.ShapeDtypeStruct((G_ROWS, EXT_COLS), BF16),
        in_specs=[smem, smem, smem, vmem, hbm, hbm],
        out_specs=vmem,
        scratch_shapes=[
            pltpu.VMEM((BLOCKS, WIN_ROWS, PTS), BF16),
            pltpu.VMEM((BLOCKS, WIN_COLS, PTS), BF16),
            pltpu.VMEM((CHUNK, 2 * WIN_ROWS, WIN_COLS), F32),
            pltpu.VMEM((4, 2, EXT_ROWS, LANES), F32),
            pltpu.SemaphoreType.DMA((2, NCHUNK)),
        ],
        compiler_params=pltpu.CompilerParams(vmem_limit_bytes=32 * MIB),
        name="spread",
    )(block_counts, theta_offsets, phi_offsets, point_values, theta_weights, phi_weights)


def split(value):
    hi = value.astype(BF16)
    return hi, (value - hi.astype(F32)).astype(BF16)


def finish_kernel(
    base, rot, twiddle, last, g_hbm, w_hbm, conv_hbm, out,
    g, w, conv, d, a, b, got_a, got_b, sum_a, sum_b, got_a2, got_b2, q, qz, r, spec,
    load_sem, conv_sem, send_a, recv_a, send_b, recv_b, send_a2, recv_a2, send_b2, recv_b2, send_z, recv_z,
):
    lat = lax.axis_index("lat")
    lon = lax.axis_index("lon")
    z_lo = lon // 16
    my = lon // 4 % 4
    mx = lon % 4
    zc = lat * 2 + z_lo

    def x_peer(by):
        to = lax.rem(mx + by, NX)
        return to, (lat, z_lo * 16 + my * 4 + to)

    def y_peer(by):
        to = lax.rem(my + by, NY)
        return to, (lat, z_lo * 16 + to * 4 + mx)

    def z_peer(by):
        to = lax.rem(zc + by, NZC)
        return to, (to // 2, to % 2 * 16 + my * 4 + mx)

    barrier = pltpu.get_barrier_semaphore()
    for peer, count in ((x_peer, NX), (y_peer, NY), (z_peer, NZC)):
        for by in range(1, count):
            pl.semaphore_signal(barrier, inc=1, device_id=peer(by)[1], device_id_type=MESH)

    half = T0 * LANES // 2
    loads = [
        pltpu.make_async_copy(g_hbm.at[pl.ds(0, half)], g.at[pl.ds(0, half)], load_sem.at[0]),
        pltpu.make_async_copy(g_hbm.at[pl.ds(half, G_ROWS - half)], g.at[pl.ds(half, G_ROWS - half)], load_sem.at[1]),
        pltpu.make_async_copy(w_hbm, w, load_sem.at[2]),
    ]
    for copy in loads:
        copy.start()
    conv_loads = [
        pltpu.make_async_copy(conv_hbm.at[0, pl.ds(k * 1024, 1024)], conv.at[pl.ds(k * 1024, 1024)], conv_sem.at[k])
        for k in range(4)
    ]
    for copy in conv_loads:
        copy.start()

    lane = lax.broadcasted_iota(jnp.int32, (ORDERS, LANES), 1)
    turn = rot[...]
    turn_cos = jnp.sum(jnp.where(lane == lon, turn, 0.0), axis=1, keepdims=True)
    turn_sin = jnp.sum(jnp.where(lane == lon + 32, turn, 0.0), axis=1, keepdims=True)
    cos, sin = base[:ORDERS, :], base[ORDERS:, :]
    here_cos = cos * turn_cos - sin * turn_sin
    here_sin = sin * turn_cos + cos * turn_sin
    cos_hi, cos_lo = split(here_cos)
    sin_hi, sin_lo = split(here_sin)
    d[0:128, :] = cos_hi
    d[128:256, :] = sin_hi
    d[256:384, :] = cos_lo
    d[384:512, :] = sin_lo

    first = lax.broadcasted_iota(jnp.int32, (ORDERS, LANES), 1) < 64

    def along(product, at):
        cut = slice(at * LANES, (at + 1) * LANES)
        by_cos = product[0:128, cut] + product[256:384, cut]
        by_sin = pltpu.roll(product[128:256, cut] + product[384:512, cut], 64, 1)
        return (by_cos + jnp.where(first, by_sin, -by_sin)).reshape(NX, NY, NZC, LANES)

    loads[0].wait()
    for pair in range(4):
        product = nt_dot(d[...], g[pair * 256 : pair * 256 + 256, :])
        for at in range(2):
            a[:, :, pair * 2 + at, :, :] = along(product, at)
    pl.semaphore_wait(barrier, (NX - 1) + (NY - 1) + (NZC - 1))

    def exchange(source, dest, peer, send, recv):
        copies = []
        for by in range(1, 4):
            to, device = peer(by)
            copies.append(pltpu.make_async_remote_copy(
                src_ref=source(to), dst_ref=dest.at[by - 1], send_sem=send.at[by - 1], recv_sem=recv.at[by - 1],
                device_id=device, device_id_type=MESH,
            ))
        for copy in copies:
            copy.start()
        return copies

    copies_a = exchange(lambda to: a.at[to], got_a, x_peer, send_a, recv_a)
    loads[1].wait()
    for pair in range(4):
        product = nt_dot(d[...], g[half + pair * 256 : half + pair * 256 + 256, :])
        for at in range(2):
            b[:, :, pair * 2 + at, :, :] = along(product, at)
    b[:, :, 8, :, :] = along(nt_dot(d[...], g[T0 * LANES : G_ROWS, :]), 0)
    copies_b = exchange(lambda to: b.at[:, to], got_b, y_peer, send_b, recv_b)

    for copy in copies_a:
        copy.wait_recv()
    sum_a[...] = (a[mx] + got_a[0]) + (got_a[1] + got_a[2])
    copies_a2 = exchange(lambda to: sum_a.at[to], got_a2, y_peer, send_a2, recv_a2)
    for copy in copies_b:
        copy.wait_recv()
    sum_b[...] = (b[:, my] + got_b[0]) + (got_b[1] + got_b[2])
    copies_b2 = exchange(lambda to: sum_b.at[to], got_b2, x_peer, send_b2, recv_b2)

    q[17 * 8 :, :] = jnp.zeros((7 * 8, LANES), F32)
    for copy in copies_a2:
        copy.wait_recv()
    q[0:64, :] = ((sum_a[my] + got_a2[0]) + (got_a2[1] + got_a2[2])).reshape(64, LANES)
    for copy in copies_b2:
        copy.wait_recv()
    q[64:136, :] = ((sum_b[mx] + got_b2[0]) + (got_b2[1] + got_b2[2])).reshape(72, LANES)
    for z in range(NZC):
        qz[z] = q[pl.ds(z, 24, stride=8), :]

    copies_z = []
    for by in range(1, NZC):
        to, device = z_peer(by)
        copies_z.append(pltpu.make_async_remote_copy(
            src_ref=qz.at[to], dst_ref=r.at[zc], send_sem=send_z.at[by - 1], recv_sem=recv_z.at[by - 1],
            device_id=device, device_id_type=MESH,
        ))
    for copy in copies_z:
        copy.start()
    r[zc] = qz[zc]
    loads[2].wait()
    for copy in copies_z:
        copy.wait_recv()

    tiles = [r[2 * i] + r[2 * i + 1] for i in range(4)]
    row = lax.broadcasted_iota(jnp.int32, (T0, LANES), 0)
    col = lax.broadcasted_iota(jnp.int32, (T0, LANES), 1)
    keep = (col % T0 == row) & (col % 64 < 32)
    margins = [jnp.where(keep, jnp.broadcast_to(tile[16:17, :], (T0, LANES)), 0.0) for tile in tiles]
    sums = jnp.concatenate([tile[0:16, :] for tile in tiles] + margins, 1)
    hi, lo = split(sums)
    both = jnp.dot(jnp.concatenate([hi, lo], 0), w[0], preferred_element_type=F32)
    inner = both[0:16] + both[16:32] + jnp.dot(hi, w[1], preferred_element_type=F32)
    real, imag = inner[:, :256], inner[:, 256:]
    cos, sin = twiddle[0:16, :], twiddle[16:32, :]
    turned = jnp.concatenate([real * cos + imag * sin, imag * cos - real * sin], 0)
    hi, lo = split(turned)
    stacked = jnp.concatenate([hi, hi, lo, jnp.zeros_like(hi)], 0)
    spectrum = jnp.dot(last[...], stacked, preferred_element_type=F32)
    hi, lo = split(spectrum)
    for side in range(2):
        cut = slice(side * LANES, (side + 1) * LANES)
        spec[side, 0:32, :] = hi[:, cut].astype(F32)
        spec[side, 32:64, :] = lo[:, cut].astype(F32)

    total = jnp.zeros((4, DEGREES), F32)
    for block in range(16):
        if block % 4 == 0:
            conv_loads[block // 4].wait()
        here = pl.ds((block + 8) % 16, 4, stride=16)
        rows = jnp.concatenate([spec[0, here, :], spec[1, here, :]], 1).astype(BF16)
        total += jnp.dot(rows, conv[block * 256 : block * 256 + 256, :], preferred_element_type=F32)
    out[0] = total[0:2] + total[2:4]

    for group in (copies_a, copies_b, copies_a2, copies_b2, copies_z):
        for copy in group:
            copy.wait_send()


def finish(g, conversion):
    base, rot, w, twiddle, last = (jnp.asarray(table) for table in tables())
    vmem = pl.BlockSpec(memory_space=pltpu.VMEM)
    hbm = pl.BlockSpec(memory_space=pl.ANY)
    dma = pltpu.SemaphoreType.DMA
    return pl.pallas_call(
        finish_kernel,
        out_shape=jax.ShapeDtypeStruct((1, 2, DEGREES), F32),
        in_specs=[vmem, vmem, vmem, vmem, hbm, hbm, hbm],
        out_specs=vmem,
        scratch_shapes=[
            pltpu.VMEM((G_ROWS, EXT_COLS), BF16),
            pltpu.VMEM((2, 1024, 512), BF16),
            pltpu.VMEM((GRID_ROWS, DEGREES), BF16),
            pltpu.VMEM((512, EXT_COLS), BF16),
            pltpu.VMEM((NX, NY, 8, NZC, LANES), F32),
            pltpu.VMEM((NX, NY, 9, NZC, LANES), F32),
            pltpu.VMEM((3, NY, 8, NZC, LANES), F32),
            pltpu.VMEM((3, NX, 9, NZC, LANES), F32),
            pltpu.VMEM((NY, 8, NZC, LANES), F32),
            pltpu.VMEM((NX, 9, NZC, LANES), F32),
            pltpu.VMEM((3, 8, NZC, LANES), F32),
            pltpu.VMEM((3, 9, NZC, LANES), F32),
            pltpu.VMEM((24 * 8, LANES), F32),
            pltpu.VMEM((NZC, 24, LANES), F32),
            pltpu.VMEM((NZC, 24, LANES), F32),
            pltpu.VMEM((2, 64, LANES), F32),
            dma((3,)), dma((4,)),
            dma((3,)), dma((3,)), dma((3,)), dma((3,)),
            dma((3,)), dma((3,)), dma((3,)), dma((3,)),
            dma((7,)), dma((7,)),
        ],
        compiler_params=pltpu.CompilerParams(
            collective_id=0, has_side_effects=True, vmem_limit_bytes=48 * MIB
        ),
        name="finish",
    )(base, rot, twiddle, last, g, w, conversion)


def shards(
    point_values, theta_weights, phi_weights, block_counts, theta_offsets, phi_offsets, conversion
):
    g = spread(point_values, theta_weights, phi_weights, block_counts, theta_offsets, phi_offsets)
    return finish(g, conversion)


def solution(mesh):
    placed = (
        P(None, ("lat", "lon"), None),
        P(("lat", "lon"), None, None),
        P(("lat", "lon"), None, None),
        P(("lat", "lon")),
        P(("lat", "lon")),
        P(("lat", "lon")),
        P(("lat", "lon"), None, None),
    )
    return jax.shard_map(
        shards, mesh=mesh, in_specs=placed, out_specs=P(("lat", "lon"), None, None), check_vma=False
    )
```

time: 587 us -> 43.7 us (0.07); the launches traced: 577 us -> 43.4 us
  matrix products: 430 us -> 0 us
  waiting for transfers between devices: 100 us -> 0 us
  Pallas kernels: 0 us -> 36.5 us
  starting transfers between devices: 16.5 us -> 0 us
  between operations: 13.9 us -> 0.08 us
  other arithmetic: 6.87 us -> 0 us
    dot_general x12 -> x0, matrix products: 430 us -> none  [the longest x1 82.5 us: theta_transform(): jnp.einsum('ct,tk->ck', sums[:, 0], sines, precision=highest)]
    unnamed x2 -> x0, waiting for transfers between devices: 36.7 us -> none
    pallas_call x0 -> x2, Pallas kernels: none -> 36.5 us  [the longest x1 29.7 us: finish(): pl.pallas_call(finish_kernel, out_shape=jax.ShapeDtypeStruct((1, 2, DEGRE...]
    all_to_all x2 -> x0, waiting for transfers between devices: 33.9 us -> none  [the longest x1 26.8 us: shards(): lax.all_to_all(tile, 'lon', split_axis=1, concat_axis=2, tiled=True)]
    ppermute x2 -> x0, waiting for transfers between devices: 29.7 us -> none  [shifted(): lax.ppermute(value, axis, [(i, (i + by) % size) for i in range(size)])]
    all_to_all x2 -> x0, starting transfers between devices: 9.87 us -> none  [the longest x1 5.69 us: shards(): lax.all_to_all(every_order, 'lon', split_axis=0, concat_axis=2, tiled=True)]
    ppermute x2 -> x0, starting transfers between devices: 6.59 us -> none  [shifted(): lax.ppermute(value, axis, [(i, (i + by) % size) for i in range(size)])]
  transfers between devices with their start and end apart: 5 -> 0, of which waited for: 5 -> 0; matrix products, arithmetic and copies ran while one was open for 0% -> 0% of each run, Pallas kernels for 0% -> 0%
where the time goes in v1:
time: 43.7 us; the launch traced here: 43.4 us
  Pallas kernels  36.5 us (84%)
  local copies, waits for them, and re-layouts  6.91 us (16%)
    pallas_call x1, Pallas kernels, finish(): pl.pallas_call(finish_kernel, out_shape=jax.ShapeDtypeStruct((1, 2, DEGRE...  29.7 us
    unnamed x23, local copies, waits for them, and re-layouts  6.91 us
    pallas_call x1, Pallas kernels, spread(): pl.pallas_call(spread_kernel, out_shape=jax.ShapeDtypeStruct((G_ROWS, EXT...  6.72 us

profile of v1, /device:TPU:1, one launch (start us, length us, event | category | flops | bytes accessed | tf_op | source)
XLA Modules:
  0.0 43.4 jit_solution(18372647917023603940)
XLA Ops:
  0.0 0.0 copy-start
  0.0 2.2 %copy-done = bf16[64,128,256]{2,1,0:T(8,128)(2,1)S(1)} copy-done((bf16[64,128,256]{2,1,0:T(8,128)(2,1)S(1)}, bf16[64,128,256]{2,1,0:T(8,128)(2,1)}, u32[]{:S(2)}) %copy-start) | copy-done | bytes 4194328
  2.2 0.0 copy-start.2
  2.2 1.2 %copy-done.2 = bf16[64,32,256]{2,1,0:T(8,128)(2,1)S(1)} copy-done((bf16[64,32,256]{2,1,0:T(8,128)(2,1)S(1)}, bf16[64,32,256]{2,1,0:T(8,128)(2,1)}, u32[]{:S(2)}) %copy-start.2) | copy-done | bytes 1048600
  3.4 0.0 copy-start.4
  3.4 0.9 %copy-done.4 = f32[2,64,256]{2,1,0:T(8,128)S(1)} copy-done((f32[2,64,256]{2,1,0:T(8,128)S(1)}, f32[2,64,256]{2,1,0:T(8,128)}, u32[]{:S(2)}) %copy-start.4) | copy-done | bytes 131096
  4.3 0.0 copy-start.8
  4.3 0.7 %copy-done.8 = s32[64]{0:T(128)S(1)} copy-done((s32[64]{0:T(128)S(1)}, s32[64]{0:T(128)}, u32[]{:S(2)}) %copy-start.8) | copy-done | bytes 280
  5.0 0.0 copy-start.9
  5.0 0.7 %copy-done.9 = s32[64]{0:T(128)S(1)} copy-done((s32[64]{0:T(128)S(1)}, s32[64]{0:T(128)}, u32[]{:S(2)}) %copy-start.9) | copy-done | bytes 280
  5.6 0.0 copy-start.10
  5.6 0.7 %copy-done.10 = s32[64]{0:T(128)S(1)} copy-done((s32[64]{0:T(128)S(1)}, s32[64]{0:T(128)}, u32[]{:S(2)}) %copy-start.10) | copy-done | bytes 280
  6.3 0.0 copy-start.1
  6.3 0.0 copy-start.3
  6.3 0.0 copy-start.5
  6.3 0.0 copy-start.6
  6.3 0.0 copy-start.7
  6.3 6.7 %spread.1.g_hbm = bf16[2176,384]{1,0:T(8,128)(2,1)S(1)} custom-call(s32[64]{0:T(128)S(1)} %copy-done.8, s32[64]{0:T(128)S(1)} %copy-done.9, s32[64]{0:T(128)S(1)} %copy-done.10, f32[2,64,256]{2,1,0:T(8,128)S(1)} %copy-done.4, bf16[64,32,256]{2,1,0:T(8,128)(2,1)S(1)} %copy-done.2, bf16[64,128,256]{2,1,0:T(8,128)(2,1)S(1)} %copy-done), custom_call_target="tpu_custom_call" | custom-call | tf_op jit(solution)/shard_map/spread/pallas_call | solution.py:148
  13.0 0.0 copy-done.1
  13.0 0.0 copy-done.3
  13.1 0.0 copy-done.5
  13.1 0.0 copy-done.6
  13.1 0.0 copy-done.7
  13.1 29.7 %finish.1 = f32[1,2,2048]{2,1,0:T(2,128)S(1)} custom-call(f32[256,384]{1,0:T(8,128)S(1)} %copy-done.3, f32[128,128]{1,0:T(8,128)S(1)} %copy-done.5, f32[32,256]{1,0:T(8,128)S(1)} %copy-done.6, bf16[32,128]{1,0:T(8,128)(2,1)S(1)} %copy-done.7, bf16[2176,384]{1,0:T(8,128)(2,1)S(1)} %spread.1.g_hbm, bf16[2,1024,512]{2,1,0:T(8,128)(2,1)S(1)} %copy-done.1, ...), custom_call_target="tpu_custom_call" | custom-call | tf_op jit(solution)/shard_map/finish/pallas_call | solution.py:337
  42.8 0.6 %copy.14 = f32[1,2,2048]{2,1,0:T(2,128)} copy(f32[1,2,2048]{2,1,0:T(2,128)S(1)} %finish.1) | data formatting | bytes 32768
Async XLA Ops:
  0.0 2.2 %copy-start = (bf16[64,128,256]{2,1,0:T(8,128)(2,1)S(1)}, bf16[64,128,256]{2,1,0:T(8,128)(2,1)}, u32[]{:S(2)}) copy-start(bf16[64,128,256]{2,1,0:T(8,128)(2,1)} %phi_hbm.1) | copy-start | bytes 12582916
  2.2 1.2 %copy-start.2 = (bf16[64,32,256]{2,1,0:T(8,128)(2,1)S(1)}, bf16[64,32,256]{2,1,0:T(8,128)(2,1)}, u32[]{:S(2)}) copy-start(bf16[64,32,256]{2,1,0:T(8,128)(2,1)} %theta_hbm.1) | copy-start | bytes 3145732
  3.4 0.9 %copy-start.4 = (f32[2,64,256]{2,1,0:T(8,128)S(1)}, f32[2,64,256]{2,1,0:T(8,128)}, u32[]{:S(2)}) copy-start(f32[2,64,256]{2,1,0:T(8,128)} %values.1) | copy-start | bytes 393220
  4.3 0.7 %copy-start.8 = (s32[64]{0:T(128)S(1)}, s32[64]{0:T(128)}, u32[]{:S(2)}) copy-start(s32[64]{0:T(128)} %counts.1) | copy-start | bytes 772
  5.0 0.7 %copy-start.9 = (s32[64]{0:T(128)S(1)}, s32[64]{0:T(128)}, u32[]{:S(2)}) copy-start(s32[64]{0:T(128)} %theta_offs.1) | copy-start | bytes 772
  5.6 0.7 %copy-start.10 = (s32[64]{0:T(128)S(1)}, s32[64]{0:T(128)}, u32[]{:S(2)}) copy-start(s32[64]{0:T(128)} %phi_offs.1) | copy-start | bytes 772
  6.3 6.8 %copy-start.1 = (bf16[2,1024,512]{2,1,0:T(8,128)(2,1)S(1)}, bf16[2,1024,512]{2,1,0:T(8,128)(2,1)}, u32[]{:S(2)}) copy-start(bf16[2,1024,512]{2,1,0:T(8,128)(2,1)} %constant.12.clone.w_hbm) | copy-start | bytes 6291460
  6.3 6.8 %copy-start.3 = (f32[256,384]{1,0:T(8,128)S(1)}, f32[256,384]{1,0:T(8,128)}, u32[]{:S(2)}) copy-start(f32[256,384]{1,0:T(8,128)} %constant.10.clone.base) | copy-start | bytes 1179652
  6.3 6.8 %copy-start.5 = (f32[128,128]{1,0:T(8,128)S(1)}, f32[128,128]{1,0:T(8,128)}, u32[]{:S(2)}) copy-start(f32[128,128]{1,0:T(8,128)} %constant.11.clone.rot) | copy-start | bytes 196612
  6.3 6.8 %copy-start.6 = (f32[32,256]{1,0:T(8,128)S(1)}, f32[32,256]{1,0:T(8,128)}, u32[]{:S(2)}) copy-start(f32[32,256]{1,0:T(8,128)} %constant.13.clone.twiddle) | copy-start | bytes 98308
  6.3 6.8 %copy-start.7 = (bf16[32,128]{1,0:T(8,128)(2,1)S(1)}, bf16[32,128]{1,0:T(8,128)(2,1)}, u32[]{:S(2)}) copy-start(bf16[32,128]{1,0:T(8,128)(2,1)} %constant.14.clone.last) | copy-start | bytes 24580

commit v2 on v1

v2 whole, which is shorter than its diff:
```python
import functools
import math

import jax
import jax.numpy as jnp
import numpy as np
from jax import lax
from jax.experimental import pallas as pl
from jax.experimental.pallas import tpu as pltpu
from jax.sharding import PartitionSpec as P

GRID_ROWS = 4096
GRID_COLS = 8192
ORDERS = 128
BLOCKS = 64
WIN_ROWS = 32
WIN_COLS = 128
PTS = 256
ROWS_DEV = 1024
COLS_DEV = 256
EXT_ROWS = ROWS_DEV + WIN_ROWS
EXT_COLS = COLS_DEV + WIN_COLS
DEGREES = 2048
LANES = 128
T0 = 64
T1 = ROWS_DEV // T0
NX, NY, NZC = 4, 4, 8
CHUNK = 8
NCHUNK = BLOCKS // CHUNK
G_ROWS = T1 * LANES + LANES
MESH = pl.DeviceIdType.MESH
MIB = 1 << 20
BF16 = jnp.bfloat16
F32 = jnp.float32


def split_np(table):
    hi = table.astype(jnp.bfloat16)
    lo = (table - hi.astype(np.float64)).astype(jnp.bfloat16)
    return hi, lo


@functools.cache
def tables():
    place = np.arange(ORDERS)
    gx, gy, zc = place // 32, place // 8 % 4, place % 8
    order = zc * 16 + gy * 4 + gx - ORDERS // 2
    phase = (order[:, None] * np.arange(EXT_COLS)[None, :]) % GRID_COLS * (2 * np.pi / GRID_COLS)
    base = np.concatenate([np.cos(phase), np.sin(phase)]).astype(np.float32)
    turn = (order[:, None] * np.arange(32)[None, :]) % 32 * (2 * np.pi / 32)
    rot = np.zeros((ORDERS, LANES), np.float32)
    rot[:, :32] = np.cos(turn)
    rot[:, 32:64] = np.sin(turn)

    index = np.arange(64)
    angle = index[:, None] * index[None, :] % 64 * (2 * np.pi / 64)
    cos, sin = np.cos(angle), np.sin(angle)
    hi, lo = split_np(np.concatenate([cos, sin]))
    first = np.concatenate([hi, lo, hi, np.zeros_like(hi)], 1)
    unitary = 1.0 / math.sqrt(GRID_ROWS * GRID_COLS)
    angle = index[:, None] * index[None, :] * (2 * np.pi / 4096)
    twiddle = np.stack([
        np.concatenate([np.cos(angle), np.cos(angle)], 1), np.concatenate([np.sin(angle), -np.sin(angle)], 1)
    ])
    twiddle = (twiddle * unitary).astype(np.float32)
    second = np.block([[cos, sin], [-sin, cos]]).reshape(2, 16, 4, 128).transpose(2, 0, 1, 3).reshape(128, 128)
    hi, lo = split_np(second)
    second = np.concatenate([hi, lo, hi], 1)
    return base, rot, first, twiddle, second


def nt_dot(a, b):
    return lax.dot_general(a, b, (((1,), (1,)), ((), ())), preferred_element_type=F32)


def spread_kernel(
    counts_hbm, theta_offs_hbm, phi_offs_hbm, base_hbm, rot_hbm, values_hbm, theta_hbm, phi_hbm, out, d,
    counts, theta_offs, phi_offs, base, rot, values, theta, phi, win_a, win_b, ext, sems, small_sems,
):
    small = [
        pltpu.make_async_copy(source, dest, small_sems.at[k])
        for k, (source, dest) in enumerate((
            (rot_hbm, rot), (base_hbm, base), (counts_hbm, counts), (theta_offs_hbm, theta_offs),
            (phi_offs_hbm, phi_offs), (values_hbm, values),
        ))
    ]
    for copy in small:
        copy.start()

    def fetch(c):
        part = pl.ds(c * CHUNK, CHUNK)
        return (
            pltpu.make_async_copy(theta_hbm.at[part], theta.at[part], sems.at[0, c]),
            pltpu.make_async_copy(phi_hbm.at[part], phi.at[part], sems.at[1, c]),
        )

    for c in range(NCHUNK):
        for copy in fetch(c):
            copy.start()

    def clear(i, carry):
        for k in range(4):
            for x in range(2):
                ext[k, x, pl.ds(pl.multiple_of(i * 96, 8), 96), :] = jnp.zeros((96, LANES), F32)
        return carry

    lax.fori_loop(0, EXT_ROWS // 96, clear, 0)

    for copy in small[:2]:
        copy.wait()
    lon = lax.axis_index("lon")
    place_of = lax.broadcasted_iota(jnp.int32, (ORDERS, LANES), 1)
    turn = rot[...]
    turn_cos = jnp.sum(jnp.where(place_of == lon, turn, 0.0), axis=1, keepdims=True)
    turn_sin = jnp.sum(jnp.where(place_of == lon + 32, turn, 0.0), axis=1, keepdims=True)
    cos, sin = base[:ORDERS, :], base[ORDERS:, :]
    cos_hi, cos_lo = split(cos * turn_cos - sin * turn_sin)
    sin_hi, sin_lo = split(sin * turn_cos + cos * turn_sin)
    d[0:128, :] = cos_hi
    d[128:256, :] = sin_hi
    d[256:384, :] = cos_lo
    d[384:512, :] = sin_lo

    point = lax.broadcasted_iota(jnp.int32, (1, PTS), 1)
    lane = lax.broadcasted_iota(jnp.int32, (WIN_ROWS, LANES), 1)

    def windows(c, win):
        for copy in fetch(c):
            copy.wait()
        for n in range(CHUNK):
            b = c * CHUNK + n
            live = point < counts[b]
            rows = theta[b].astype(F32)
            parts = []
            for x in range(2):
                own = jnp.where(live, values[x, pl.ds(b, 1), :], 0.0)
                parts.append((rows * own).astype(BF16))
            win[n] = nt_dot(jnp.concatenate(parts, 0), phi[b])

    def place(c, win):
        for n in range(CHUNK):
            b = c * CHUNK + n
            row = theta_offs[b]
            col = phi_offs[b]
            tile = col // LANES
            shift = col % LANES
            near = lane >= shift
            here = pl.ds(row, WIN_ROWS)
            for x in range(2):
                moved = pltpu.roll(win[n, x * WIN_ROWS : (x + 1) * WIN_ROWS, :], shift, 1)
                ext[tile, x, here, :] += jnp.where(near, moved, 0.0)
                ext[tile + 1, x, here, :] += jnp.where(near, 0.0, moved)

    for copy in small[2:]:
        copy.wait()
    windows(0, win_a)

    def step(i, carry):
        windows(2 * i + 1, win_b)
        place(2 * i, win_a)
        windows(2 * i + 2, win_a)
        place(2 * i + 1, win_b)
        return carry

    lax.fori_loop(0, NCHUNK // 2 - 1, step, 0)
    windows(NCHUNK - 1, win_b)
    place(NCHUNK - 2, win_a)
    place(NCHUNK - 1, win_b)

    for k in range(3):
        cols = slice(k * LANES, (k + 1) * LANES)
        for x in range(2):
            for t1 in range(T1):
                at = t1 * LANES + x * T0
                out[at : at + T0, cols] = ext[k, x, t1 * T0 : (t1 + 1) * T0, :].astype(BF16)
            at = T1 * LANES + x * T0
            out[at : at + 32, cols] = ext[k, x, ROWS_DEV:EXT_ROWS, :].astype(BF16)
            out[at + 32 : at + 64, cols] = jnp.zeros((32, LANES), BF16)


def spread(point_values, theta_weights, phi_weights, block_counts, theta_offsets, phi_offsets):
    base, rot = (jnp.asarray(table) for table in tables()[:2])
    vmem = pl.BlockSpec(memory_space=pltpu.VMEM)
    operands = [block_counts, theta_offsets, phi_offsets, base, rot, point_values, theta_weights, phi_weights]
    return pl.pallas_call(
        spread_kernel,
        out_shape=(
            jax.ShapeDtypeStruct((G_ROWS, EXT_COLS), BF16),
            jax.ShapeDtypeStruct((4 * ORDERS, EXT_COLS), BF16),
        ),
        in_specs=[pl.BlockSpec(memory_space=pltpu.HBM)] * len(operands),
        out_specs=(vmem, vmem),
        scratch_shapes=[
            pltpu.SMEM((BLOCKS,), jnp.int32),
            pltpu.SMEM((BLOCKS,), jnp.int32),
            pltpu.SMEM((BLOCKS,), jnp.int32),
            pltpu.VMEM((2 * ORDERS, EXT_COLS), F32),
            pltpu.VMEM((ORDERS, LANES), F32),
            pltpu.VMEM((2, BLOCKS, PTS), F32),
            pltpu.VMEM((BLOCKS, WIN_ROWS, PTS), BF16),
            pltpu.VMEM((BLOCKS, WIN_COLS, PTS), BF16),
            pltpu.VMEM((CHUNK, 2 * WIN_ROWS, WIN_COLS), F32),
            pltpu.VMEM((CHUNK, 2 * WIN_ROWS, WIN_COLS), F32),
            pltpu.VMEM((4, 2, EXT_ROWS, LANES), F32),
            pltpu.SemaphoreType.DMA((2, NCHUNK)),
            pltpu.SemaphoreType.DMA((6,)),
        ],
        compiler_params=pltpu.CompilerParams(vmem_limit_bytes=32 * MIB),
        name="spread",
    )(*(pltpu.with_memory_space_constraint(operand, pltpu.HBM) for operand in operands))


def split(value):
    hi = value.astype(BF16)
    return hi, (value - hi.astype(F32)).astype(BF16)


def finish_kernel(
    g, d, first, twiddle, second, conv_hbm, out,
    conv, a, b, got_a, got_b, sum_a, sum_b, got_a2, got_b2, q, qz, r, spec,
    conv_sem, send_a, recv_a, send_b, recv_b, send_a2, recv_a2, send_b2, recv_b2, send_z, recv_z,
):
    lat = lax.axis_index("lat")
    lon = lax.axis_index("lon")
    z_lo = lon // 16
    my = lon // 4 % 4
    mx = lon % 4
    zc = lat * 2 + z_lo

    def x_peer(by):
        to = lax.rem(mx + by, NX)
        return to, (lat, z_lo * 16 + my * 4 + to)

    def y_peer(by):
        to = lax.rem(my + by, NY)
        return to, (lat, z_lo * 16 + to * 4 + mx)

    def z_peer(by):
        to = lax.rem(zc + by, NZC)
        return to, (to // 2, to % 2 * 16 + my * 4 + mx)

    barrier = pltpu.get_barrier_semaphore()
    for peer, count in ((x_peer, NX), (y_peer, NY), (z_peer, NZC)):
        for by in range(1, count):
            pl.semaphore_signal(barrier, inc=1, device_id=peer(by)[1], device_id_type=MESH)

    half = T1 * LANES // 2
    conv_loads = [
        pltpu.make_async_copy(conv_hbm.at[0, pl.ds(k * 1024, 1024)], conv.at[pl.ds(k * 1024, 1024)], conv_sem.at[k])
        for k in range(4)
    ]
    for copy in conv_loads:
        copy.start()

    early = lax.broadcasted_iota(jnp.int32, (ORDERS, LANES), 1) < 64

    def along(product, at):
        cut = slice(at * LANES, (at + 1) * LANES)
        by_cos = product[0:128, cut] + product[256:384, cut]
        by_sin = pltpu.roll(product[128:256, cut] + product[384:512, cut], 64, 1)
        return (by_cos + jnp.where(early, by_sin, -by_sin)).reshape(NX, NY, NZC, LANES)

    for pair in range(4):
        product = nt_dot(d[...], g[pair * 256 : pair * 256 + 256, :])
        for at in range(2):
            a[:, :, pair * 2 + at, :, :] = along(product, at)
    pl.semaphore_wait(barrier, (NX - 1) + (NY - 1) + (NZC - 1))

    def exchange(source, dest, peer, send, recv):
        copies = []
        for by in range(1, 4):
            to, device = peer(by)
            copies.append(pltpu.make_async_remote_copy(
                src_ref=source(to), dst_ref=dest.at[by - 1], send_sem=send.at[by - 1], recv_sem=recv.at[by - 1],
                device_id=device, device_id_type=MESH,
            ))
        for copy in copies:
            copy.start()
        return copies

    copies_a = exchange(lambda to: a.at[to], got_a, x_peer, send_a, recv_a)
    for pair in range(4):
        product = nt_dot(d[...], g[half + pair * 256 : half + pair * 256 + 256, :])
        for at in range(2):
            b[:, :, pair * 2 + at, :, :] = along(product, at)
    b[:, :, 8, :, :] = along(nt_dot(d[...], g[T1 * LANES : G_ROWS, :]), 0)
    copies_b = exchange(lambda to: b.at[:, to], got_b, y_peer, send_b, recv_b)

    for copy in copies_a:
        copy.wait_recv()
    sum_a[...] = (a[mx] + got_a[0]) + (got_a[1] + got_a[2])
    copies_a2 = exchange(lambda to: sum_a.at[to], got_a2, y_peer, send_a2, recv_a2)
    for copy in copies_b:
        copy.wait_recv()
    sum_b[...] = (b[:, my] + got_b[0]) + (got_b[1] + got_b[2])
    copies_b2 = exchange(lambda to: sum_b.at[to], got_b2, x_peer, send_b2, recv_b2)

    q[17 * 8 :, :] = jnp.zeros((7 * 8, LANES), F32)
    for copy in copies_a2:
        copy.wait_recv()
    q[0:64, :] = ((sum_a[my] + got_a2[0]) + (got_a2[1] + got_a2[2])).reshape(64, LANES)
    for copy in copies_b2:
        copy.wait_recv()
    q[64:136, :] = ((sum_b[mx] + got_b2[0]) + (got_b2[1] + got_b2[2])).reshape(72, LANES)
    for z in range(NZC):
        qz[z] = q[pl.ds(z, 24, stride=8), :]

    copies_z = []
    for by in range(1, NZC):
        to, device = z_peer(by)
        copies_z.append(pltpu.make_async_remote_copy(
            src_ref=qz.at[to], dst_ref=r.at[zc], send_sem=send_z.at[by - 1], recv_sem=recv_z.at[by - 1],
            device_id=device, device_id_type=MESH,
        ))
    for copy in copies_z:
        copy.start()
    r[zc] = qz[zc]
    for copy in copies_z:
        copy.wait_recv()

    tiles = [r[2 * i] + r[2 * i + 1] for i in range(4)]
    top = lax.broadcasted_iota(jnp.int32, (T1, LANES), 0) == 0
    rows = [
        tile[0:T1, :] + jnp.where(top, jnp.broadcast_to(above[T1 : T1 + 1, :], (T1, LANES)), 0.0)
        for tile, above in zip(tiles, tiles[3:] + tiles[:3])
    ]
    hi, lo = split(jnp.concatenate(rows, 0))
    both = jnp.dot(first[...], jnp.concatenate([hi, hi, lo, jnp.zeros_like(hi)], 0), preferred_element_type=F32)
    by_sin = pltpu.roll(both[64:128], 64, 1)
    inner = both[0:64] + jnp.where(early[0:64], by_sin, -by_sin)
    turned = inner * twiddle[0] + pltpu.roll(inner, 64, 1) * twiddle[1]
    hi, lo = split(turned)
    parts = nt_dot(second[...], jnp.concatenate([hi, hi, lo], 1))
    hi, lo = split(jnp.concatenate([parts[32 * j : 32 * j + 32] for j in range(4)], 1))
    for side in range(2):
        cut = slice(side * LANES, (side + 1) * LANES)
        spec[side, 0:32, :] = hi[:, cut].astype(F32)
        spec[side, 32:64, :] = lo[:, cut].astype(F32)

    total = jnp.zeros((4, DEGREES), F32)
    for block in range(16):
        if block % 4 == 0:
            conv_loads[block // 4].wait()
        here = pl.ds((block + 8) % 16, 4, stride=16)
        rows = jnp.concatenate([spec[0, here, :], spec[1, here, :]], 1).astype(BF16)
        total += jnp.dot(rows, conv[block * 256 : block * 256 + 256, :], preferred_element_type=F32)
    out[0] = total[0:2] + total[2:4]

    for group in (copies_a, copies_b, copies_a2, copies_b2, copies_z):
        for copy in group:
            copy.wait_send()


def finish(g, d, conversion):
    first, twiddle, second = (jnp.asarray(table) for table in tables()[2:])
    vmem = pl.BlockSpec(memory_space=pltpu.VMEM)
    hbm = pl.BlockSpec(memory_space=pl.ANY)
    dma = pltpu.SemaphoreType.DMA
    return pl.pallas_call(
        finish_kernel,
        out_shape=jax.ShapeDtypeStruct((1, 2, DEGREES), F32),
        in_specs=[vmem, vmem, vmem, vmem, vmem, hbm],
        out_specs=vmem,
        scratch_shapes=[
            pltpu.VMEM((GRID_ROWS, DEGREES), BF16),
            pltpu.VMEM((NX, NY, 8, NZC, LANES), F32),
            pltpu.VMEM((NX, NY, 9, NZC, LANES), F32),
            pltpu.VMEM((3, NY, 8, NZC, LANES), F32),
            pltpu.VMEM((3, NX, 9, NZC, LANES), F32),
            pltpu.VMEM((NY, 8, NZC, LANES), F32),
            pltpu.VMEM((NX, 9, NZC, LANES), F32),
            pltpu.VMEM((3, 8, NZC, LANES), F32),
            pltpu.VMEM((3, 9, NZC, LANES), F32),
            pltpu.VMEM((24 * 8, LANES), F32),
            pltpu.VMEM((NZC, 24, LANES), F32),
            pltpu.VMEM((NZC, 24, LANES), F32),
            pltpu.VMEM((2, 64, LANES), F32),
            dma((4,)),
            dma((3,)), dma((3,)), dma((3,)), dma((3,)),
            dma((3,)), dma((3,)), dma((3,)), dma((3,)),
            dma((7,)), dma((7,)),
        ],
        compiler_params=pltpu.CompilerParams(
            collective_id=0, has_side_effects=True, vmem_limit_bytes=48 * MIB
        ),
        name="finish",
    )(g, d, first, twiddle, second, conversion)


def shards(
    point_values, theta_weights, phi_weights, block_counts, theta_offsets, phi_offsets, conversion
):
    g, d = spread(point_values, theta_weights, phi_weights, block_counts, theta_offsets, phi_offsets)
    return finish(g, d, conversion)


def solution(mesh):
    placed = (
        P(None, ("lat", "lon"), None),
        P(("lat", "lon"), None, None),
        P(("lat", "lon"), None, None),
        P(("lat", "lon")),
        P(("lat", "lon")),
        P(("lat", "lon")),
        P(("lat", "lon"), None, None),
    )
    return jax.shard_map(
        shards, mesh=mesh, in_specs=placed, out_specs=P(("lat", "lon"), None, None), check_vma=False
    )
```

time: 43.7 us -> 35 us (0.80)
  local copies, waits for them, and re-layouts: 6.91 us -> 0.62 us
  Pallas kernels: 36.5 us -> 34.3 us
    unnamed x23 -> x7, local copies, waits for them, and re-layouts: 6.91 us -> 0.62 us
    pallas_call x1, Pallas kernels: 6.72 us -> 5.45 us  [spread(): pl.pallas_call(spread_kernel, out_shape=(jax.ShapeDtypeStruct((G_ROWS, EX...]
    pallas_call x1, Pallas kernels: 29.7 us -> 28.8 us  [finish(): pl.pallas_call(finish_kernel, out_shape=jax.ShapeDtypeStruct((1, 2, DEGRE...]
where the time goes in v2:
time: 35 us; the launch traced here: 34.9 us
  Pallas kernels  34.3 us (98%)
  local copies, waits for them, and re-layouts  0.62 us (2%)
    pallas_call x1, Pallas kernels, finish(): pl.pallas_call(finish_kernel, out_shape=jax.ShapeDtypeStruct((1, 2, DEGRE...  28.8 us
    pallas_call x1, Pallas kernels, spread(): pl.pallas_call(spread_kernel, out_shape=(jax.ShapeDtypeStruct((G_ROWS, EX...  5.45 us

profile of v2, /device:TPU:1, one launch (start us, length us, event | category | flops | bytes accessed | tf_op | source)
XLA Modules:
  0.0 34.9 jit_solution(16045377523838188712)
XLA Ops:
  0.0 0.0 copy-start
  0.0 0.0 copy-start.1
  0.0 0.0 copy-start.2
  0.0 5.4 %spread.1 = (bf16[2176,384]{1,0:T(8,128)(2,1)S(1)}, bf16[512,384]{1,0:T(8,128)(2,1)S(1)}) custom-call(s32[64]{0:T(128)} %counts_hbm.1, s32[64]{0:T(128)} %theta_offs_hbm.1, s32[64]{0:T(128)} %phi_offs_hbm.1, f32[256,384]{1,0:T(8,128)} %constant.10.clone.base_hbm, f32[128,128]{1,0:T(8,128)} %constant.11.clone.rot_hbm, f32[2,64,256]{2,1,0:T(8,128)} %values_hbm.1, ...), custom_call_target="tpu_custom_call" | custom-call | tf_op jit(solution)/shard_map/spread/pallas_call | solution.py:185
  5.5 0.0 copy-done
  5.5 0.0 copy-done.1
  5.5 0.0 copy-done.2
  5.5 28.8 %finish.1 = f32[1,2,2048]{2,1,0:T(2,128)S(1)} custom-call(bf16[2176,384]{1,0:T(8,128)(2,1)S(1)} %get-tuple-element.7.g, bf16[512,384]{1,0:T(8,128)(2,1)S(1)} %get-tuple-element.8.d, bf16[128,256]{1,0:T(8,128)(2,1)S(1)} %copy-done.2, f32[2,64,128]{2,1,0:T(8,128)S(1)} %copy-done.1, bf16[128,384]{1,0:T(8,128)(2,1)S(1)} %copy-done, bf16[1,4096,2048]{2,1,0:T(8,128)(2,1)} %conv_hbm.1), custom_call_target="tpu_custom_call" | custom-call | tf_op jit(solution)/shard_map/finish/pallas_call | solution.py:359
  34.3 0.6 %copy.14 = f32[1,2,2048]{2,1,0:T(2,128)} copy(f32[1,2,2048]{2,1,0:T(2,128)S(1)} %finish.1) | data formatting | bytes 32768
Async XLA Ops:
  0.0 5.5 %copy-start = (bf16[128,384]{1,0:T(8,128)(2,1)S(1)}, bf16[128,384]{1,0:T(8,128)(2,1)}, u32[]{:S(2)}) copy-start(bf16[128,384]{1,0:T(8,128)(2,1)} %constant.14.clone.second) | copy-start | bytes 294916
  0.0 5.5 %copy-start.1 = (f32[2,64,128]{2,1,0:T(8,128)S(1)}, f32[2,64,128]{2,1,0:T(8,128)}, u32[]{:S(2)}) copy-start(f32[2,64,128]{2,1,0:T(8,128)} %constant.13.clone.twiddle) | copy-start | bytes 196612
  0.0 5.5 %copy-start.2 = (bf16[128,256]{1,0:T(8,128)(2,1)S(1)}, bf16[128,256]{1,0:T(8,128)(2,1)}, u32[]{:S(2)}) copy-start(bf16[128,256]{1,0:T(8,128)(2,1)} %constant.12.clone.first) | copy-start | bytes 196612

commit v3 on v2

--- a/solution.py
+++ b/solution.py
@@ -94,7 +94,7 @@
             pltpu.make_async_copy(phi_hbm.at[part], phi.at[part], sems.at[1, c]),
         )
 
-    for c in range(NCHUNK):
+    for c in range(4):
         for copy in fetch(c):
             copy.start()
 
@@ -125,6 +125,11 @@
     lane = lax.broadcasted_iota(jnp.int32, (WIN_ROWS, LANES), 1)
 
     def windows(c, win):
+        @pl.when(c + 4 < NCHUNK)
+        def _():
+            for copy in fetch(c + 4):
+                copy.start()
+
         for copy in fetch(c):
             copy.wait()
         for n in range(CHUNK):
@@ -205,7 +210,7 @@
             pltpu.SemaphoreType.DMA((2, NCHUNK)),
             pltpu.SemaphoreType.DMA((6,)),
         ],
-        compiler_params=pltpu.CompilerParams(vmem_limit_bytes=32 * MIB),
+        compiler_params=pltpu.CompilerParams(vmem_limit_bytes=24 * MIB),
         name="spread",
     )(*(pltpu.with_memory_space_constraint(operand, pltpu.HBM) for operand in operands))
 
@@ -216,8 +221,9 @@
 
 
 def finish_kernel(
-    g, d, first, twiddle, second, conv_hbm, out,
-    conv, a, b, got_a, got_b, sum_a, sum_b, got_a2, got_b2, q, qz, r, spec,
+    g, d, first_hbm, twiddle_hbm, second_hbm, conv_hbm, out, conv,
+    a, b, got_a, got_b, relay_a, relay_b, on_a, on_b, sum_a, sum_b, got_a2, got_b2,
+    q, qz_a, qz_b, r_a, r_b, first, twiddle, second,
     conv_sem, send_a, recv_a, send_b, recv_b, send_a2, recv_a2, send_b2, recv_b2, send_z, recv_z,
 ):
     lat = lax.axis_index("lat")
@@ -246,9 +252,15 @@
 
     half = T1 * LANES // 2
     conv_loads = [
-        pltpu.make_async_copy(conv_hbm.at[0, pl.ds(k * 1024, 1024)], conv.at[pl.ds(k * 1024, 1024)], conv_sem.at[k])
+        pltpu.make_async_copy(conv_hbm.at[0, pl.ds(k * 1024, 1024)], conv.at[0, pl.ds(k * 1024, 1024)], conv_sem.at[k])
         for k in range(4)
     ]
+    table_loads = [
+        pltpu.make_async_copy(source, dest, conv_sem.at[4 + k])
+        for k, (source, dest) in enumerate(((first_hbm, first), (twiddle_hbm, twiddle), (second_hbm, second)))
+    ]
+    for copy in table_loads:
+        copy.start()
     for copy in conv_loads:
         copy.start()
 
@@ -264,65 +276,108 @@
         product = nt_dot(d[...], g[pair * 256 : pair * 256 + 256, :])
         for at in range(2):
             a[:, :, pair * 2 + at, :, :] = along(product, at)
+    for pair in range(4):
+        product = nt_dot(d[...], g[half + pair * 256 : half + pair * 256 + 256, :])
+        for at in range(2):
+            b[:, :, pair * 2 + at, :, :] = along(product, at)
+    b[:, :, 8, :, :] = along(nt_dot(d[...], g[T1 * LANES : G_ROWS, :]), 0)
     pl.semaphore_wait(barrier, (NX - 1) + (NY - 1) + (NZC - 1))
+
+    def ring(part, peer, relay, on, got, send, recv):
+        (ahead, ahead_id), (across, _), (behind, behind_id) = peer(1), peer(2), peer(3)
+
+        def copy(k, source, dest, device):
+            return pltpu.make_async_remote_copy(
+                src_ref=source, dst_ref=dest, send_sem=send.at[k], recv_sem=recv.at[k],
+                device_id=device, device_id_type=MESH,
+            )
+
+        low, high = pl.ds(0, 2), pl.ds(2, 2)
+        copies = [
+            copy(0, part(across, low), relay.at[0], ahead_id),
+            copy(1, part(across, high), relay.at[1], behind_id),
+            copy(2, part(ahead, high), got.at[0, high], ahead_id),
+            copy(3, part(behind, low), got.at[1, low], behind_id),
+            copy(4, on.at[0], got.at[0, low], ahead_id),
+            copy(5, on.at[1], got.at[1, high], behind_id),
+        ]
+        for one in copies[:4]:
+            one.start()
+
+        def pass_on():
+            copies[0].wait_recv()
+            on[0] = part(ahead, low)[...] + relay[0]
+            copies[4].start()
+            copies[1].wait_recv()
+            on[1] = part(behind, high)[...] + relay[1]
+            copies[5].start()
+
+        return copies, pass_on
+
+    copies_a, pass_on_a = ring(lambda to, side: a.at[to, side], x_peer, relay_a, on_a, got_a, send_a, recv_a)
+    copies_b, pass_on_b = ring(lambda to, side: b.at[side, to], y_peer, relay_b, on_b, got_b, send_b, recv_b)
+    pass_on_a()
+    pass_on_b()
 
     def exchange(source, dest, peer, send, recv):
         copies = []
         for by in range(1, 4):
             to, device = peer(by)
             copies.append(pltpu.make_async_remote_copy(
-                src_ref=source(to), dst_ref=dest.at[by - 1], send_sem=send.at[by - 1], recv_sem=recv.at[by - 1],
+                src_ref=source.at[to], dst_ref=dest.at[by - 1], send_sem=send.at[by - 1], recv_sem=recv.at[by - 1],
                 device_id=device, device_id_type=MESH,
             ))
         for copy in copies:
             copy.start()
         return copies
 
-    copies_a = exchange(lambda to: a.at[to], got_a, x_peer, send_a, recv_a)
-    for pair in range(4):
-        product = nt_dot(d[...], g[half + pair * 256 : half + pair * 256 + 256, :])
-        for at in range(2):
-            b[:, :, pair * 2 + at, :, :] = along(product, at)
-    b[:, :, 8, :, :] = along(nt_dot(d[...], g[T1 * LANES : G_ROWS, :]), 0)
-    copies_b = exchange(lambda to: b.at[:, to], got_b, y_peer, send_b, recv_b)
-
-    for copy in copies_a:
+    for copy in copies_a[2:]:
         copy.wait_recv()
-    sum_a[...] = (a[mx] + got_a[0]) + (got_a[1] + got_a[2])
-    copies_a2 = exchange(lambda to: sum_a.at[to], got_a2, y_peer, send_a2, recv_a2)
-    for copy in copies_b:
+    sum_a[...] = a[mx] + got_a[0] + got_a[1]
+    copies_a2 = exchange(sum_a, got_a2, y_peer, send_a2, recv_a2)
+    for copy in copies_b[2:]:
         copy.wait_recv()
-    sum_b[...] = (b[:, my] + got_b[0]) + (got_b[1] + got_b[2])
-    copies_b2 = exchange(lambda to: sum_b.at[to], got_b2, x_peer, send_b2, recv_b2)
+    sum_b[...] = b[:, my] + got_b[0] + got_b[1]
+    copies_b2 = exchange(sum_b, got_b2, x_peer, send_b2, recv_b2)
+
+    def deliver(source, dest, row):
+        copies = []
+        for by in range(1, NZC):
+            to, device = z_peer(by)
+            copies.append(pltpu.make_async_remote_copy(
+                src_ref=source.at[to], dst_ref=dest.at[zc],
+                send_sem=send_z.at[row, by - 1], recv_sem=recv_z.at[row, by - 1],
+                device_id=device, device_id_type=MESH,
+            ))
+        for copy in copies:
+            copy.start()
+        dest[zc] = source[zc]
+        return copies
 
     q[17 * 8 :, :] = jnp.zeros((7 * 8, LANES), F32)
     for copy in copies_a2:
         copy.wait_recv()
     q[0:64, :] = ((sum_a[my] + got_a2[0]) + (got_a2[1] + got_a2[2])).reshape(64, LANES)
+    for z in range(NZC):
+        qz_a[z] = q[pl.ds(z, 8, stride=8), :]
+    copies_za = deliver(qz_a, r_a, 0)
     for copy in copies_b2:
         copy.wait_recv()
     q[64:136, :] = ((sum_b[mx] + got_b2[0]) + (got_b2[1] + got_b2[2])).reshape(72, LANES)
     for z in range(NZC):
-        qz[z] = q[pl.ds(z, 24, stride=8), :]
-
-    copies_z = []
-    for by in range(1, NZC):
-        to, device = z_peer(by)
-        copies_z.append(pltpu.make_async_remote_copy(
-            src_ref=qz.at[to], dst_ref=r.at[zc], send_sem=send_z.at[by - 1], recv_sem=recv_z.at[by - 1],
-            device_id=device, device_id_type=MESH,
-        ))
-    for copy in copies_z:
-        copy.start()
-    r[zc] = qz[zc]
-    for copy in copies_z:
+        qz_b[z] = q[pl.ds(64 + z, 16, stride=8), :]
+    copies_zb = deliver(qz_b, r_b, 1)
+    for copy in copies_za + copies_zb:
         copy.wait_recv()
 
-    tiles = [r[2 * i] + r[2 * i + 1] for i in range(4)]
+    for copy in table_loads:
+        copy.wait()
+    later = [r_b[2 * i] + r_b[2 * i + 1] for i in range(4)]
     top = lax.broadcasted_iota(jnp.int32, (T1, LANES), 0) == 0
     rows = [
-        tile[0:T1, :] + jnp.where(top, jnp.broadcast_to(above[T1 : T1 + 1, :], (T1, LANES)), 0.0)
-        for tile, above in zip(tiles, tiles[3:] + tiles[:3])
+        jnp.concatenate([r_a[2 * i] + r_a[2 * i + 1], later[i][0:8, :]], 0)
+        + jnp.where(top, jnp.broadcast_to(later[i - 1][8:9, :], (T1, LANES)), 0.0)
+        for i in range(4)
     ]
     hi, lo = split(jnp.concatenate(rows, 0))
     both = jnp.dot(first[...], jnp.concatenate([hi, hi, lo, jnp.zeros_like(hi)], 0), preferred_element_type=F32)
@@ -334,19 +389,12 @@
     hi, lo = split(jnp.concatenate([parts[32 * j : 32 * j + 32] for j in range(4)], 1))
     for side in range(2):
         cut = slice(side * LANES, (side + 1) * LANES)
-        spec[side, 0:32, :] = hi[:, cut].astype(F32)
-        spec[side, 32:64, :] = lo[:, cut].astype(F32)
-
-    total = jnp.zeros((4, DEGREES), F32)
-    for block in range(16):
-        if block % 4 == 0:
-            conv_loads[block // 4].wait()
-        here = pl.ds((block + 8) % 16, 4, stride=16)
-        rows = jnp.concatenate([spec[0, here, :], spec[1, here, :]], 1).astype(BF16)
-        total += jnp.dot(rows, conv[block * 256 : block * 256 + 256, :], preferred_element_type=F32)
-    out[0] = total[0:2] + total[2:4]
-
-    for group in (copies_a, copies_b, copies_a2, copies_b2, copies_z):
+        out[side, 0:32, :] = hi[:, cut].astype(F32)
+        out[side, 32:64, :] = lo[:, cut].astype(F32)
+
+    for copy in conv_loads:
+        copy.wait()
+    for group in (copies_a, copies_b, copies_a2, copies_b2, copies_za, copies_zb):
         for copy in group:
             copy.wait_send()
 
@@ -354,44 +402,75 @@
 def finish(g, d, conversion):
     first, twiddle, second = (jnp.asarray(table) for table in tables()[2:])
     vmem = pl.BlockSpec(memory_space=pltpu.VMEM)
-    hbm = pl.BlockSpec(memory_space=pl.ANY)
     dma = pltpu.SemaphoreType.DMA
     return pl.pallas_call(
         finish_kernel,
-        out_shape=jax.ShapeDtypeStruct((1, 2, DEGREES), F32),
-        in_specs=[vmem, vmem, vmem, vmem, vmem, hbm],
-        out_specs=vmem,
+        out_shape=(
+            jax.ShapeDtypeStruct((2, 64, LANES), F32),
+            jax.ShapeDtypeStruct((1, GRID_ROWS, DEGREES), BF16),
+        ),
+        in_specs=[vmem, vmem] + [pl.BlockSpec(memory_space=pltpu.HBM)] * 4,
+        out_specs=(vmem, vmem),
         scratch_shapes=[
-            pltpu.VMEM((GRID_ROWS, DEGREES), BF16),
             pltpu.VMEM((NX, NY, 8, NZC, LANES), F32),
             pltpu.VMEM((NX, NY, 9, NZC, LANES), F32),
-            pltpu.VMEM((3, NY, 8, NZC, LANES), F32),
-            pltpu.VMEM((3, NX, 9, NZC, LANES), F32),
+            pltpu.VMEM((2, NY, 8, NZC, LANES), F32),
+            pltpu.VMEM((2, NX, 9, NZC, LANES), F32),
+            pltpu.VMEM((2, 2, 8, NZC, LANES), F32),
+            pltpu.VMEM((2, 2, 9, NZC, LANES), F32),
+            pltpu.VMEM((2, 2, 8, NZC, LANES), F32),
+            pltpu.VMEM((2, 2, 9, NZC, LANES), F32),
             pltpu.VMEM((NY, 8, NZC, LANES), F32),
             pltpu.VMEM((NX, 9, NZC, LANES), F32),
             pltpu.VMEM((3, 8, NZC, LANES), F32),
             pltpu.VMEM((3, 9, NZC, LANES), F32),
             pltpu.VMEM((24 * 8, LANES), F32),
-            pltpu.VMEM((NZC, 24, LANES), F32),
-            pltpu.VMEM((NZC, 24, LANES), F32),
+            pltpu.VMEM((NZC, 8, LANES), F32),
+            pltpu.VMEM((NZC, 16, LANES), F32),
+            pltpu.VMEM((NZC, 8, LANES), F32),
+            pltpu.VMEM((NZC, 16, LANES), F32),
+            pltpu.VMEM((128, 256), BF16),
             pltpu.VMEM((2, 64, LANES), F32),
-            dma((4,)),
+            pltpu.VMEM((128, 384), BF16),
+            dma((7,)),
+            dma((6,)), dma((6,)), dma((6,)), dma((6,)),
             dma((3,)), dma((3,)), dma((3,)), dma((3,)),
-            dma((3,)), dma((3,)), dma((3,)), dma((3,)),
-            dma((7,)), dma((7,)),
+            dma((2, 7)), dma((2, 7)),
         ],
         compiler_params=pltpu.CompilerParams(
-            collective_id=0, has_side_effects=True, vmem_limit_bytes=48 * MIB
+            collective_id=0, has_side_effects=True, vmem_limit_bytes=20 * MIB
         ),
         name="finish",
-    )(g, d, first, twiddle, second, conversion)
+    )(g, d, *(pltpu.with_memory_space_constraint(operand, pltpu.HBM) for operand in (first, twiddle, second, conversion)))
+
+
+def convert_kernel(spec, conv, out):
+    total = jnp.zeros((4, DEGREES), F32)
+    for block in range(16):
+        here = pl.ds((block + 8) % 16, 4, stride=16)
+        rows = jnp.concatenate([spec[0, here, :], spec[1, here, :]], 1).astype(BF16)
+        part = conv[0, block * 256 : block * 256 + 256, :]
+        total += jnp.dot(rows, part, preferred_element_type=F32)
+    out[0] = total[0:2] + total[2:4]
+
+
+def convert(spec, conversion):
+    vmem = pl.BlockSpec(memory_space=pltpu.VMEM)
+    return pl.pallas_call(
+        convert_kernel,
+        out_shape=jax.ShapeDtypeStruct((1, 2, DEGREES), F32),
+        in_specs=[vmem, vmem],
+        out_specs=vmem,
+        compiler_params=pltpu.CompilerParams(vmem_limit_bytes=24 * MIB),
+        name="convert",
+    )(spec, conversion)
 
 
 def shards(
     point_values, theta_weights, phi_weights, block_counts, theta_offsets, phi_offsets, conversion
 ):
     g, d = spread(point_values, theta_weights, phi_weights, block_counts, theta_offsets, phi_offsets)
-    return finish(g, d, conversion)
+    return convert(*finish(g, d, conversion))
 
 
 def solution(mesh):

time: 35 us -> 32.7 us (0.934)
  Pallas kernels: 34.3 us -> 32.5 us
  local copies, waits for them, and re-layouts: 0.62 us -> 0 us
    pallas_call x1 -> x2, Pallas kernels: 28.8 us -> 27.9 us  [the longest x1 25 us: finish(): pl.pallas_call(finish_kernel, out_shape=(jax.ShapeDtypeStruct((2, 64, LAN...]
    pallas_call x1, Pallas kernels: 5.45 us -> 4.63 us  [spread(): pl.pallas_call(spread_kernel, out_shape=(jax.ShapeDtypeStruct((G_ROWS, EX...]
    unnamed x7 -> x0, local copies, waits for them, and re-layouts: 0.62 us -> none
where the time goes in v3:
time: 32.7 us; the launch traced here: 32.5 us
  Pallas kernels  32.5 us (99%)
    pallas_call x1, Pallas kernels, finish(): pl.pallas_call(finish_kernel, out_shape=(jax.ShapeDtypeStruct((2, 64, LAN...  25 us
    pallas_call x1, Pallas kernels, spread(): pl.pallas_call(spread_kernel, out_shape=(jax.ShapeDtypeStruct((G_ROWS, EX...  4.63 us
    pallas_call x1, Pallas kernels, convert(): pl.pallas_call(convert_kernel, out_shape=jax.ShapeDtypeStruct((1, 2, DEGR...  2.88 us

profile of v3, /device:TPU:1, one launch (start us, length us, event | category | flops | bytes accessed | tf_op | source)
XLA Modules:
  0.0 32.5 jit_solution(2877409512505939637)
XLA Ops:
  0.0 4.6 %spread.1 = (bf16[2176,384]{1,0:T(8,128)(2,1)S(1)}, bf16[512,384]{1,0:T(8,128)(2,1)S(1)}) custom-call(s32[64]{0:T(128)} %counts_hbm.1, s32[64]{0:T(128)} %theta_offs_hbm.1, s32[64]{0:T(128)} %phi_offs_hbm.1, f32[256,384]{1,0:T(8,128)} %constant.10.clone.base_hbm, f32[128,128]{1,0:T(8,128)} %constant.11.clone.rot_hbm, f32[2,64,256]{2,1,0:T(8,128)} %values_hbm.1, ...), custom_call_target="tpu_custom_call" | custom-call | tf_op jit(solution)/shard_map/spread/pallas_call | solution.py:190
  4.6 25.0 %finish.1 = (f32[2,64,128]{2,1,0:T(8,128)S(1)}, bf16[1,4096,2048]{2,1,0:T(8,128)(2,1)S(1)}) custom-call(bf16[2176,384]{1,0:T(8,128)(2,1)S(1)} %get-tuple-element.9.g, bf16[512,384]{1,0:T(8,128)(2,1)S(1)} %get-tuple-element.10.d, bf16[128,256]{1,0:T(8,128)(2,1)} %constant.12.clone.first_hbm, f32[2,64,128]{2,1,0:T(8,128)} %constant.13.clone.twiddle_hbm, ...), custom_call_target="tpu_custom_call" | custom-call | tf_op jit(solution)/shard_map/finish/pallas_call | solution.py:406
  29.7 2.9 %convert.1 = f32[1,2,2048]{2,1,0:T(2,128)} custom-call(f32[2,64,128]{2,1,0:T(8,128)S(1)} %get-tuple-element.11.spec, bf16[1,4096,2048]{2,1,0:T(8,128)(2,1)S(1)} %get-tuple-element.12.conv), custom_call_target="tpu_custom_call" | custom-call | tf_op jit(solution)/shard_map/convert/pallas_call | solution.py:459

commit v4 on v3

--- a/solution.py
+++ b/solution.py
@@ -25,7 +25,7 @@
 T0 = 64
 T1 = ROWS_DEV // T0
 NX, NY, NZC = 4, 4, 8
-CHUNK = 8
+CHUNK = 16
 NCHUNK = BLOCKS // CHUNK
 G_ROWS = T1 * LANES + LANES
 MESH = pl.DeviceIdType.MESH
@@ -48,9 +48,10 @@
     phase = (order[:, None] * np.arange(EXT_COLS)[None, :]) % GRID_COLS * (2 * np.pi / GRID_COLS)
     base = np.concatenate([np.cos(phase), np.sin(phase)]).astype(np.float32)
     turn = (order[:, None] * np.arange(32)[None, :]) % 32 * (2 * np.pi / 32)
-    rot = np.zeros((ORDERS, LANES), np.float32)
-    rot[:, :32] = np.cos(turn)
-    rot[:, 32:64] = np.sin(turn)
+    rot = np.zeros((2 * ORDERS, LANES), np.float32)
+    rot[:ORDERS, :32] = np.cos(turn)
+    rot[:ORDERS, 32:64] = np.sin(turn)
+    base = np.concatenate([base, rot], 1)
 
     index = np.arange(64)
     angle = index[:, None] * index[None, :] % 64 * (2 * np.pi / 64)
@@ -66,7 +67,7 @@
     second = np.block([[cos, sin], [-sin, cos]]).reshape(2, 16, 4, 128).transpose(2, 0, 1, 3).reshape(128, 128)
     hi, lo = split_np(second)
     second = np.concatenate([hi, lo, hi], 1)
-    return base, rot, first, twiddle, second
+    return base, first, twiddle, second
 
 
 def nt_dot(a, b):
@@ -74,14 +75,14 @@
 
 
 def spread_kernel(
-    counts_hbm, theta_offs_hbm, phi_offs_hbm, base_hbm, rot_hbm, values_hbm, theta_hbm, phi_hbm, out, d,
-    counts, theta_offs, phi_offs, base, rot, values, theta, phi, win_a, win_b, ext, sems, small_sems,
+    counts_hbm, theta_offs_hbm, phi_offs_hbm, base_hbm, values_hbm, theta_hbm, phi_hbm, out, d,
+    counts, theta_offs, phi_offs, base, values, theta, phi, win_a, win_b, ext, sems, small_sems,
 ):
     small = [
         pltpu.make_async_copy(source, dest, small_sems.at[k])
         for k, (source, dest) in enumerate((
-            (rot_hbm, rot), (base_hbm, base), (counts_hbm, counts), (theta_offs_hbm, theta_offs),
-            (phi_offs_hbm, phi_offs), (values_hbm, values),
+            (base_hbm, base), (counts_hbm, counts), (values_hbm, values),
+            (theta_offs_hbm, theta_offs), (phi_offs_hbm, phi_offs),
         ))
     ]
     for copy in small:
@@ -94,7 +95,7 @@
             pltpu.make_async_copy(phi_hbm.at[part], phi.at[part], sems.at[1, c]),
         )
 
-    for c in range(4):
+    for c in range(3):
         for copy in fetch(c):
             copy.start()
 
@@ -106,14 +107,13 @@
 
     lax.fori_loop(0, EXT_ROWS // 96, clear, 0)
 
-    for copy in small[:2]:
-        copy.wait()
+    small[0].wait()
     lon = lax.axis_index("lon")
     place_of = lax.broadcasted_iota(jnp.int32, (ORDERS, LANES), 1)
-    turn = rot[...]
+    turn = base[:ORDERS, EXT_COLS:]
     turn_cos = jnp.sum(jnp.where(place_of == lon, turn, 0.0), axis=1, keepdims=True)
     turn_sin = jnp.sum(jnp.where(place_of == lon + 32, turn, 0.0), axis=1, keepdims=True)
-    cos, sin = base[:ORDERS, :], base[ORDERS:, :]
+    cos, sin = base[:ORDERS, :EXT_COLS], base[ORDERS:, :EXT_COLS]
     cos_hi, cos_lo = split(cos * turn_cos - sin * turn_sin)
     sin_hi, sin_lo = split(sin * turn_cos + cos * turn_sin)
     d[0:128, :] = cos_hi
@@ -125,9 +125,9 @@
     lane = lax.broadcasted_iota(jnp.int32, (WIN_ROWS, LANES), 1)
 
     def windows(c, win):
-        @pl.when(c + 4 < NCHUNK)
+        @pl.when(c + 3 < NCHUNK)
         def _():
-            for copy in fetch(c + 4):
+            for copy in fetch(c + 3):
                 copy.start()
 
         for copy in fetch(c):
@@ -156,7 +156,7 @@
                 ext[tile, x, here, :] += jnp.where(near, moved, 0.0)
                 ext[tile + 1, x, here, :] += jnp.where(near, 0.0, moved)
 
-    for copy in small[2:]:
+    for copy in small[1:]:
         copy.wait()
     windows(0, win_a)
 
@@ -184,9 +184,9 @@
 
 
 def spread(point_values, theta_weights, phi_weights, block_counts, theta_offsets, phi_offsets):
-    base, rot = (jnp.asarray(table) for table in tables()[:2])
+    base = jnp.asarray(tables()[0])
     vmem = pl.BlockSpec(memory_space=pltpu.VMEM)
-    operands = [block_counts, theta_offsets, phi_offsets, base, rot, point_values, theta_weights, phi_weights]
+    operands = [block_counts, theta_offsets, phi_offsets, base, point_values, theta_weights, phi_weights]
     return pl.pallas_call(
         spread_kernel,
         out_shape=(
@@ -199,8 +199,7 @@
             pltpu.SMEM((BLOCKS,), jnp.int32),
             pltpu.SMEM((BLOCKS,), jnp.int32),
             pltpu.SMEM((BLOCKS,), jnp.int32),
-            pltpu.VMEM((2 * ORDERS, EXT_COLS), F32),
-            pltpu.VMEM((ORDERS, LANES), F32),
+            pltpu.VMEM((2 * ORDERS, EXT_COLS + LANES), F32),
             pltpu.VMEM((2, BLOCKS, PTS), F32),
             pltpu.VMEM((BLOCKS, WIN_ROWS, PTS), BF16),
             pltpu.VMEM((BLOCKS, WIN_COLS, PTS), BF16),
@@ -208,7 +207,7 @@
             pltpu.VMEM((CHUNK, 2 * WIN_ROWS, WIN_COLS), F32),
             pltpu.VMEM((4, 2, EXT_ROWS, LANES), F32),
             pltpu.SemaphoreType.DMA((2, NCHUNK)),
-            pltpu.SemaphoreType.DMA((6,)),
+            pltpu.SemaphoreType.DMA((5,)),
         ],
         compiler_params=pltpu.CompilerParams(vmem_limit_bytes=24 * MIB),
         name="spread",
@@ -246,9 +245,9 @@
         return to, (to // 2, to % 2 * 16 + my * 4 + mx)
 
     barrier = pltpu.get_barrier_semaphore()
-    for peer, count in ((x_peer, NX), (y_peer, NY), (z_peer, NZC)):
-        for by in range(1, count):
-            pl.semaphore_signal(barrier, inc=1, device_id=peer(by)[1], device_id_type=MESH)
+    far_first = [(z_peer, by) for by in (4, 3, 5, 1, 7, 2, 6)] + [(peer, by) for by in (2, 1, 3) for peer in (x_peer, y_peer)]
+    for peer, by in far_first:
+        pl.semaphore_signal(barrier, inc=1, device_id=peer(by)[1], device_id_type=MESH)
 
     half = T1 * LANES // 2
     conv_loads = [
@@ -280,7 +279,7 @@
         product = nt_dot(d[...], g[half + pair * 256 : half + pair * 256 + 256, :])
         for at in range(2):
             b[:, :, pair * 2 + at, :, :] = along(product, at)
-    b[:, :, 8, :, :] = along(nt_dot(d[...], g[T1 * LANES : G_ROWS, :]), 0)
+    a[:, :, 8, :, :] = along(nt_dot(d[...], g[T1 * LANES : G_ROWS, :]), 0)
     pl.semaphore_wait(barrier, (NX - 1) + (NY - 1) + (NZC - 1))
 
     def ring(part, peer, relay, on, got, send, recv):
@@ -301,9 +300,6 @@
             copy(4, on.at[0], got.at[0, low], ahead_id),
             copy(5, on.at[1], got.at[1, high], behind_id),
         ]
-        for one in copies[:4]:
-            one.start()
-
         def pass_on():
             copies[0].wait_recv()
             on[0] = part(ahead, low)[...] + relay[0]
@@ -316,6 +312,8 @@
 
     copies_a, pass_on_a = ring(lambda to, side: a.at[to, side], x_peer, relay_a, on_a, got_a, send_a, recv_a)
     copies_b, pass_on_b = ring(lambda to, side: b.at[side, to], y_peer, relay_b, on_b, got_b, send_b, recv_b)
+    for one in copies_a[:2] + copies_b[:2] + copies_a[2:4] + copies_b[2:4]:
+        one.start()
     pass_on_a()
     pass_on_b()
 
@@ -354,29 +352,29 @@
         dest[zc] = source[zc]
         return copies
 
-    q[17 * 8 :, :] = jnp.zeros((7 * 8, LANES), F32)
+    q[72:128, :] = jnp.zeros((56, LANES), F32)
     for copy in copies_a2:
         copy.wait_recv()
-    q[0:64, :] = ((sum_a[my] + got_a2[0]) + (got_a2[1] + got_a2[2])).reshape(64, LANES)
+    q[0:72, :] = ((sum_a[my] + got_a2[0]) + (got_a2[1] + got_a2[2])).reshape(72, LANES)
     for z in range(NZC):
-        qz_a[z] = q[pl.ds(z, 8, stride=8), :]
+        qz_a[z] = q[pl.ds(z, 16, stride=8), :]
     copies_za = deliver(qz_a, r_a, 0)
     for copy in copies_b2:
         copy.wait_recv()
-    q[64:136, :] = ((sum_b[mx] + got_b2[0]) + (got_b2[1] + got_b2[2])).reshape(72, LANES)
+    q[128:192, :] = ((sum_b[mx] + got_b2[0]) + (got_b2[1] + got_b2[2])).reshape(64, LANES)
     for z in range(NZC):
-        qz_b[z] = q[pl.ds(64 + z, 16, stride=8), :]
+        qz_b[z] = q[pl.ds(128 + z, 8, stride=8), :]
     copies_zb = deliver(qz_b, r_b, 1)
     for copy in copies_za + copies_zb:
         copy.wait_recv()
 
     for copy in table_loads:
         copy.wait()
-    later = [r_b[2 * i] + r_b[2 * i + 1] for i in range(4)]
+    first_rows = [r_a[2 * i] + r_a[2 * i + 1] for i in range(4)]
     top = lax.broadcasted_iota(jnp.int32, (T1, LANES), 0) == 0
     rows = [
-        jnp.concatenate([r_a[2 * i] + r_a[2 * i + 1], later[i][0:8, :]], 0)
-        + jnp.where(top, jnp.broadcast_to(later[i - 1][8:9, :], (T1, LANES)), 0.0)
+        jnp.concatenate([first_rows[i][0:8, :], r_b[2 * i] + r_b[2 * i + 1]], 0)
+        + jnp.where(top, jnp.broadcast_to(first_rows[i - 1][8:9, :], (T1, LANES)), 0.0)
         for i in range(4)
     ]
     hi, lo = split(jnp.concatenate(rows, 0))
@@ -400,7 +398,7 @@
 
 
 def finish(g, d, conversion):
-    first, twiddle, second = (jnp.asarray(table) for table in tables()[2:])
+    first, twiddle, second = (jnp.asarray(table) for table in tables()[1:])
     vmem = pl.BlockSpec(memory_space=pltpu.VMEM)
     dma = pltpu.SemaphoreType.DMA
     return pl.pallas_call(
@@ -412,23 +410,23 @@
         in_specs=[vmem, vmem] + [pl.BlockSpec(memory_space=pltpu.HBM)] * 4,
         out_specs=(vmem, vmem),
         scratch_shapes=[
+            pltpu.VMEM((NX, NY, 9, NZC, LANES), F32),
             pltpu.VMEM((NX, NY, 8, NZC, LANES), F32),
-            pltpu.VMEM((NX, NY, 9, NZC, LANES), F32),
-            pltpu.VMEM((2, NY, 8, NZC, LANES), F32),
-            pltpu.VMEM((2, NX, 9, NZC, LANES), F32),
+            pltpu.VMEM((2, NY, 9, NZC, LANES), F32),
+            pltpu.VMEM((2, NX, 8, NZC, LANES), F32),
+            pltpu.VMEM((2, 2, 9, NZC, LANES), F32),
             pltpu.VMEM((2, 2, 8, NZC, LANES), F32),
             pltpu.VMEM((2, 2, 9, NZC, LANES), F32),
             pltpu.VMEM((2, 2, 8, NZC, LANES), F32),
-            pltpu.VMEM((2, 2, 9, NZC, LANES), F32),
-            pltpu.VMEM((NY, 8, NZC, LANES), F32),
-            pltpu.VMEM((NX, 9, NZC, LANES), F32),
+            pltpu.VMEM((NY, 9, NZC, LANES), F32),
+            pltpu.VMEM((NX, 8, NZC, LANES), F32),
+            pltpu.VMEM((3, 9, NZC, LANES), F32),
             pltpu.VMEM((3, 8, NZC, LANES), F32),
-            pltpu.VMEM((3, 9, NZC, LANES), F32),
             pltpu.VMEM((24 * 8, LANES), F32),
+            pltpu.VMEM((NZC, 16, LANES), F32),
             pltpu.VMEM((NZC, 8, LANES), F32),
             pltpu.VMEM((NZC, 16, LANES), F32),
             pltpu.VMEM((NZC, 8, LANES), F32),
-            pltpu.VMEM((NZC, 16, LANES), F32),
             pltpu.VMEM((128, 256), BF16),
             pltpu.VMEM((2, 64, LANES), F32),
             pltpu.VMEM((128, 384), BF16),

time: 32.7 us -> 31.9 us (0.976)
  Pallas kernels: 32.5 us -> 31.8 us
    pallas_call x1, Pallas kernels: 4.63 us -> 4 us  [spread(): pl.pallas_call(spread_kernel, out_shape=(jax.ShapeDtypeStruct((G_ROWS, EX...]
where the time goes in v4:
time: 31.9 us; the launch traced here: 31.8 us
  Pallas kernels  31.8 us (100%)
    pallas_call x1, Pallas kernels, finish(): pl.pallas_call(finish_kernel, out_shape=(jax.ShapeDtypeStruct((2, 64, LAN...  24.9 us
    pallas_call x1, Pallas kernels, spread(): pl.pallas_call(spread_kernel, out_shape=(jax.ShapeDtypeStruct((G_ROWS, EX...  4 us
    pallas_call x1, Pallas kernels, convert(): pl.pallas_call(convert_kernel, out_shape=jax.ShapeDtypeStruct((1, 2, DEGR...  2.88 us

profile of v4, /device:TPU:1, one launch (start us, length us, event | category | flops | bytes accessed | tf_op | source)
XLA Modules:
  0.0 31.8 jit_solution(8006407408360920195)
XLA Ops:
  0.0 4.0 %spread.1 = (bf16[2176,384]{1,0:T(8,128)(2,1)S(1)}, bf16[512,384]{1,0:T(8,128)(2,1)S(1)}) custom-call(s32[64]{0:T(128)} %counts_hbm.1, s32[64]{0:T(128)} %theta_offs_hbm.1, s32[64]{0:T(128)} %phi_offs_hbm.1, f32[256,512]{1,0:T(8,128)} %constant.8.clone.base_hbm, f32[2,64,256]{2,1,0:T(8,128)} %values_hbm.1, bf16[64,32,256]{2,1,0:T(8,128)(2,1)} %theta_hbm.1, ...), custom_call_target="tpu_custom_call" | custom-call | tf_op jit(solution)/shard_map/spread/pallas_call | solution.py:190
  4.0 24.9 %finish.1 = (f32[2,64,128]{2,1,0:T(8,128)S(1)}, bf16[1,4096,2048]{2,1,0:T(8,128)(2,1)S(1)}) custom-call(bf16[2176,384]{1,0:T(8,128)(2,1)S(1)} %get-tuple-element.9.g, bf16[512,384]{1,0:T(8,128)(2,1)S(1)} %get-tuple-element.10.d, bf16[128,256]{1,0:T(8,128)(2,1)} %constant.9.clone.first_hbm, f32[2,64,128]{2,1,0:T(8,128)} %constant.10.clone.twiddle_hbm, ...), custom_call_target="tpu_custom_call" | custom-call | tf_op jit(solution)/shard_map/finish/pallas_call | solution.py:404
  28.9 2.9 %convert.1 = f32[1,2,2048]{2,1,0:T(2,128)} custom-call(f32[2,64,128]{2,1,0:T(8,128)S(1)} %get-tuple-element.11.spec, bf16[1,4096,2048]{2,1,0:T(8,128)(2,1)S(1)} %get-tuple-element.12.conv), custom_call_target="tpu_custom_call" | custom-call | tf_op jit(solution)/shard_map/convert/pallas_call | solution.py:457

commit v5 on v4

--- a/solution.py
+++ b/solution.py
@@ -90,14 +90,17 @@
 
     def fetch(c):
         part = pl.ds(c * CHUNK, CHUNK)
-        return (
-            pltpu.make_async_copy(theta_hbm.at[part], theta.at[part], sems.at[0, c]),
-            pltpu.make_async_copy(phi_hbm.at[part], phi.at[part], sems.at[1, c]),
-        )
-
-    for c in range(3):
-        for copy in fetch(c):
-            copy.start()
+        return pltpu.make_async_copy(phi_hbm.at[part], phi.at[part], sems.at[0, c])
+
+    def fetch_rows(k):
+        part = (pl.ds(0, CHUNK), pl.ds(CHUNK, BLOCKS - CHUNK))[k]
+        return pltpu.make_async_copy(theta_hbm.at[part], theta.at[part], sems.at[1, k])
+
+    fetch_rows(0).start()
+    fetch(0).start()
+    fetch(1).start()
+    fetch_rows(1).start()
+    fetch(2).start()
 
     def clear(i, carry):
         for k in range(4):
@@ -127,11 +130,9 @@
     def windows(c, win):
         @pl.when(c + 3 < NCHUNK)
         def _():
-            for copy in fetch(c + 3):
-                copy.start()
-
-        for copy in fetch(c):
-            copy.wait()
+            fetch(c + 3).start()
+
+        fetch(c).wait()
         for n in range(CHUNK):
             b = c * CHUNK + n
             live = point < counts[b]
@@ -158,7 +159,9 @@
 
     for copy in small[1:]:
         copy.wait()
+    fetch_rows(0).wait()
     windows(0, win_a)
+    fetch_rows(1).wait()
 
     def step(i, carry):
         windows(2 * i + 1, win_b)
@@ -251,8 +254,8 @@
 
     half = T1 * LANES // 2
     conv_loads = [
-        pltpu.make_async_copy(conv_hbm.at[0, pl.ds(k * 1024, 1024)], conv.at[0, pl.ds(k * 1024, 1024)], conv_sem.at[k])
-        for k in range(4)
+        pltpu.make_async_copy(conv_hbm, conv, conv_sem.at[k])
+        for k in range(1)
     ]
     table_loads = [
         pltpu.make_async_copy(source, dest, conv_sem.at[4 + k])
@@ -319,7 +322,7 @@
 
     def exchange(source, dest, peer, send, recv):
         copies = []
-        for by in range(1, 4):
+        for by in (2, 1, 3):
             to, device = peer(by)
             copies.append(pltpu.make_async_remote_copy(
                 src_ref=source.at[to], dst_ref=dest.at[by - 1], send_sem=send.at[by - 1], recv_sem=recv.at[by - 1],
@@ -340,7 +343,7 @@
 
     def deliver(source, dest, row):
         copies = []
-        for by in range(1, NZC):
+        for by in (4, 3, 5, 1, 7, 2, 6):
             to, device = z_peer(by)
             copies.append(pltpu.make_async_remote_copy(
                 src_ref=source.at[to], dst_ref=dest.at[zc],
@@ -365,11 +368,14 @@
     for z in range(NZC):
         qz_b[z] = q[pl.ds(128 + z, 8, stride=8), :]
     copies_zb = deliver(qz_b, r_b, 1)
+    for group in (copies_a, copies_b, copies_a2, copies_b2, copies_za):
+        for copy in group:
+            copy.wait_send()
+    for copy in table_loads + conv_loads:
+        copy.wait()
     for copy in copies_za + copies_zb:
         copy.wait_recv()
 
-    for copy in table_loads:
-        copy.wait()
     first_rows = [r_a[2 * i] + r_a[2 * i + 1] for i in range(4)]
     top = lax.broadcasted_iota(jnp.int32, (T1, LANES), 0) == 0
     rows = [
@@ -390,11 +396,8 @@
         out[side, 0:32, :] = hi[:, cut].astype(F32)
         out[side, 32:64, :] = lo[:, cut].astype(F32)
 
-    for copy in conv_loads:
-        copy.wait()
-    for group in (copies_a, copies_b, copies_a2, copies_b2, copies_za, copies_zb):
-        for copy in group:
-            copy.wait_send()
+    for copy in copies_zb:
+        copy.wait_send()
 
 
 def finish(g, d, conversion):

time: 31.9 us -> 31.5 us (0.987)
  Pallas kernels: 31.8 us -> 31.4 us
    pallas_call x1, Pallas kernels: 24.9 us -> 24.6 us  [finish(): pl.pallas_call(finish_kernel, out_shape=(jax.ShapeDtypeStruct((2, 64, LAN...]
where the time goes in v5:
time: 31.5 us; the launch traced here: 31.4 us
  Pallas kernels  31.4 us (100%)
    pallas_call x1, Pallas kernels, finish(): pl.pallas_call(finish_kernel, out_shape=(jax.ShapeDtypeStruct((2, 64, LAN...  24.6 us
    pallas_call x1, Pallas kernels, spread(): pl.pallas_call(spread_kernel, out_shape=(jax.ShapeDtypeStruct((G_ROWS, EX...  3.95 us
    pallas_call x1, Pallas kernels, convert(): pl.pallas_call(convert_kernel, out_shape=jax.ShapeDtypeStruct((1, 2, DEGR...  2.88 us

profile of v5, /device:TPU:1, one launch (start us, length us, event | category | flops | bytes accessed | tf_op | source)
XLA Modules:
  0.0 31.4 jit_solution(1216983472333163995)
XLA Ops:
  0.0 4.0 %spread.1 = (bf16[2176,384]{1,0:T(8,128)(2,1)S(1)}, bf16[512,384]{1,0:T(8,128)(2,1)S(1)}) custom-call(s32[64]{0:T(128)} %counts_hbm.1, s32[64]{0:T(128)} %theta_offs_hbm.1, s32[64]{0:T(128)} %phi_offs_hbm.1, f32[256,512]{1,0:T(8,128)} %constant.8.clone.base_hbm, f32[2,64,256]{2,1,0:T(8,128)} %values_hbm.1, bf16[64,32,256]{2,1,0:T(8,128)(2,1)} %theta_hbm.1, ...), custom_call_target="tpu_custom_call" | custom-call | tf_op jit(solution)/shard_map/spread/pallas_call | solution.py:193
  4.0 24.6 %finish.1 = (f32[2,64,128]{2,1,0:T(8,128)S(1)}, bf16[1,4096,2048]{2,1,0:T(8,128)(2,1)S(1)}) custom-call(bf16[2176,384]{1,0:T(8,128)(2,1)S(1)} %get-tuple-element.9.g, bf16[512,384]{1,0:T(8,128)(2,1)S(1)} %get-tuple-element.10.d, bf16[128,256]{1,0:T(8,128)(2,1)} %constant.9.clone.first_hbm, f32[2,64,128]{2,1,0:T(8,128)} %constant.10.clone.twiddle_hbm, ...), custom_call_target="tpu_custom_call" | custom-call | tf_op jit(solution)/shard_map/finish/pallas_call | solution.py:407
  28.5 2.9 %convert.1 = f32[1,2,2048]{2,1,0:T(2,128)} custom-call(f32[2,64,128]{2,1,0:T(8,128)S(1)} %get-tuple-element.11.spec, bf16[1,4096,2048]{2,1,0:T(8,128)(2,1)S(1)} %get-tuple-element.12.conv), custom_call_target="tpu_custom_call" | custom-call | tf_op jit(solution)/shard_map/convert/pallas_call | solution.py:460

commit v6 on v5

--- a/solution.py
+++ b/solution.py
@@ -356,6 +356,7 @@
         return copies
 
     q[72:128, :] = jnp.zeros((56, LANES), F32)
+    out[:, 64:128, :] = jnp.zeros((2, 64, LANES), F32)
     for copy in copies_a2:
         copy.wait_recv()
     q[0:72, :] = ((sum_a[my] + got_a2[0]) + (got_a2[1] + got_a2[2])).reshape(72, LANES)
@@ -407,7 +408,7 @@
     return pl.pallas_call(
         finish_kernel,
         out_shape=(
-            jax.ShapeDtypeStruct((2, 64, LANES), F32),
+            jax.ShapeDtypeStruct((2, 128, LANES), F32),
             jax.ShapeDtypeStruct((1, GRID_ROWS, DEGREES), BF16),
         ),
         in_specs=[vmem, vmem] + [pl.BlockSpec(memory_space=pltpu.HBM)] * 4,
@@ -446,9 +447,9 @@
 
 
 def convert_kernel(spec, conv, out):
-    total = jnp.zeros((4, DEGREES), F32)
+    total = jnp.zeros((8, DEGREES), F32)
     for block in range(16):
-        here = pl.ds((block + 8) % 16, 4, stride=16)
+        here = pl.ds((block + 8) % 16, 8, stride=16)
         rows = jnp.concatenate([spec[0, here, :], spec[1, here, :]], 1).astype(BF16)
         part = conv[0, block * 256 : block * 256 + 256, :]
         total += jnp.dot(rows, part, preferred_element_type=F32)

time: 31.5 us -> 31.5 us (level)
  no operation moved by 1% of the time
where the time goes in v6:
time: 31.5 us; the launch traced here: 31.4 us
  Pallas kernels  31.4 us (100%)
    pallas_call x1, Pallas kernels, finish(): pl.pallas_call(finish_kernel, out_shape=(jax.ShapeDtypeStruct((2, 128, LA...  24.6 us
    pallas_call x1, Pallas kernels, spread(): pl.pallas_call(spread_kernel, out_shape=(jax.ShapeDtypeStruct((G_ROWS, EX...  3.95 us
    pallas_call x1, Pallas kernels, convert(): pl.pallas_call(convert_kernel, out_shape=jax.ShapeDtypeStruct((1, 2, DEGR...  2.88 us

profile of v6, /device:TPU:1, one launch (start us, length us, event | category | flops | bytes accessed | tf_op | source)
XLA Modules:
  0.0 31.4 jit_solution(8928818782410114674)
XLA Ops:
  0.0 4.0 %spread.1 = (bf16[2176,384]{1,0:T(8,128)(2,1)S(1)}, bf16[512,384]{1,0:T(8,128)(2,1)S(1)}) custom-call(s32[64]{0:T(128)} %counts_hbm.1, s32[64]{0:T(128)} %theta_offs_hbm.1, s32[64]{0:T(128)} %phi_offs_hbm.1, f32[256,512]{1,0:T(8,128)} %constant.8.clone.base_hbm, f32[2,64,256]{2,1,0:T(8,128)} %values_hbm.1, bf16[64,32,256]{2,1,0:T(8,128)(2,1)} %theta_hbm.1, ...), custom_call_target="tpu_custom_call" | custom-call | tf_op jit(solution)/shard_map/spread/pallas_call | solution.py:193
  4.0 24.6 %finish.1 = (f32[2,128,128]{2,1,0:T(8,128)S(1)}, bf16[1,4096,2048]{2,1,0:T(8,128)(2,1)S(1)}) custom-call(bf16[2176,384]{1,0:T(8,128)(2,1)S(1)} %get-tuple-element.9.g, bf16[512,384]{1,0:T(8,128)(2,1)S(1)} %get-tuple-element.10.d, bf16[128,256]{1,0:T(8,128)(2,1)} %constant.9.clone.first_hbm, f32[2,64,128]{2,1,0:T(8,128)} %constant.10.clone.twiddle_hbm, ...), custom_call_target="tpu_custom_call" | custom-call | tf_op jit(solution)/shard_map/finish/pallas_call | solution.py:408
  28.6 2.9 %convert.1 = f32[1,2,2048]{2,1,0:T(2,128)} custom-call(f32[2,128,128]{2,1,0:T(8,128)S(1)} %get-tuple-element.11.spec, bf16[1,4096,2048]{2,1,0:T(8,128)(2,1)S(1)} %get-tuple-element.12.conv), custom_call_target="tpu_custom_call" | custom-call | tf_op jit(solution)/shard_map/convert/pallas_call | solution.py:461
